TPU v7x, 32 devices: a whole 2x2x4 slice. The times are simulated.
32 devices in a mesh: groups: 2 (over x), cluster: 16 (over z, y, core).
Axes of the slice: x: 2, y: 2, z: 4, core: 2. Of those that a mesh axis runs over, the one named last changes fastest.
Arguments:
- embed: bfloat16 [32768, 768], P(('groups', 'cluster')), parts along dimension 0, may hold values from -6 to 6
- valid: int32 [32768], P(('groups', 'cluster')), parts along dimension 0, may hold values from 0 to 1, as said below
- pairs: int32 [224, 2], P(('groups', 'cluster')), parts along dimension 0, may hold values from 0 to 31, as said below
- pair_count: int32 [32], P(('groups', 'cluster')), parts along dimension 0, may hold values from 1 to 7, as said below
Outputs:
- log_density: float32 [32768], P(('groups', 'cluster')), parts along dimension 0
- neighbour_sum: bfloat16 [32768, 768], P(('groups', 'cluster')), parts along dimension 0
There are 2 independent parts, one for each index of `groups`. A program takes and returns all parts, laid end to end along the dimension named above; each array names one. Nothing has to cross between parts.
Inputs may be any that keep to these rules, and one draw needn't show every extreme that they name: `pairs`: clusters are runs of 1 to 4 consecutive blocks. The live slots of index d list, each once, every pair (i, j) with i <= j of blocks of one cluster whose first block i is held by d (i // 2 == d); so j // 2 - d is 0 to 2, and this bound is reached. Dead slots hold arbitrary blocks of d. `pair_count`: some index has all 7 slots live. `valid`: in each block the real rows come first and there is at least one; only the last block of a cluster has padding.
All inputs are finite; a program needn't handle non-finite values.
Results may differ from a plain program's by a relative error of at most 0.007.
Values may be sent and summed in bfloat16 or wider, within the bound.
No kernel may reach another device: no remote copies, remote signals or barrier semaphores. Data moves between devices by JAX's collectives and lax.ppermute only.
A program may use at most 64 MiB of HBM per device.

v0:
```python
import functools

import jax
import jax.numpy as jnp
from jax import lax
from jax.experimental import pallas as pl
from jax.experimental.pallas import tpu as pltpu
from jax.sharding import PartitionSpec as P

BLOCK = 512
HALF = BLOCK // 2
TILE = 16
LANES = 128
MARK = 100.0
SHARPNESS = 8.0
LOG2E = 1.4426950408889634

IDX, PAR, V0, V1, E0, E1, C0, C1 = range(8)

VM = pl.BlockSpec(memory_space=pltpu.VMEM)
SM = pl.BlockSpec(memory_space=pltpu.SMEM)
HB = pl.BlockSpec(memory_space=pltpu.HBM)


def iota(shape, dim):
    return lax.broadcasted_iota(jnp.int32, shape, dim)


def normalized(rows):
    wide = rows.astype(jnp.float32)
    scale = lax.rsqrt(jnp.mean(wide * wide, axis=-1, keepdims=True) + 1e-06)
    return wide * scale


def marked(rows, count):
    mark = jnp.where(iota(rows.shape, 1) == 0, MARK, 0.0)
    return jnp.where(iota(rows.shape, 0) < count, rows, mark).astype(jnp.bfloat16)


def real_rows(ref, start, rows):
    head = ref[pl.ds(start, rows), 0:LANES].astype(jnp.float32)
    real = jnp.logical_and(iota(head.shape, 1) == 0, head < 0.5 * MARK)
    return jnp.sum(jnp.where(real, 1.0, 0.0)).astype(jnp.int32)


def at(block):
    return pl.multiple_of(block * BLOCK, BLOCK)


def kernel_tile(left, right, count):
    gram = lax.dot_general(
        left, right, (((1,), (1,)), ((), ())), preferred_element_type=jnp.float32
    )
    scale = SHARPNESS * LOG2E / left.shape[1]
    kern = jnp.exp2(gram * scale - SHARPNESS * LOG2E)
    return jnp.where(iota(kern.shape, 1) < count, kern, 0.0)


def folded(kern):
    return functools.reduce(
        jnp.add, [kern[:, c : c + LANES] for c in range(0, kern.shape[1], LANES)]
    )


def terms(left, right, count):
    kern = kernel_tile(left, right, count)
    sums = jnp.dot(kern.astype(jnp.bfloat16), right, preferred_element_type=jnp.float32)
    return folded(kern), sums


def add_terms(x_ref, starts, rights, dens_ref, acc_ref):
    kerns = [
        [kernel_tile(x_ref[pl.ds(start, BLOCK), :], right, count) for right, count in rights]
        for start in starts
    ]
    for start, row in zip(starts, kerns):
        place = pl.ds(start, BLOCK)
        dens_ref[place, :] += functools.reduce(jnp.add, [folded(kern) for kern in row])
        sums = [
            jnp.dot(kern.astype(jnp.bfloat16), right, preferred_element_type=jnp.float32)
            for kern, (right, _) in zip(row, rights)
        ]
        acc_ref[place, :] += functools.reduce(jnp.add, sums)


def add_linked(s, start, other, x_ref, rights, dens_ref, acc_ref):
    @pl.when(s[E0] == 1)
    def _():
        add_terms(x_ref, (start, other), rights, dens_ref, acc_ref)

    @pl.when(s[E0] == 0)
    def _():
        add_terms(x_ref, (start,), rights, dens_ref, acc_ref)


def sibling_links(s, sib_ref):
    tile = sib_ref[pl.ds(2 * BLOCK, TILE), 0:LANES].astype(jnp.float32)
    lane = iota(tile.shape, 1)
    inner = jnp.max(jnp.where(lane == 0, tile, 0.0)) > 0.5
    outer = jnp.max(jnp.where(lane == 1, tile, 0.0)) > 0.5
    return inner, outer


def joined(s, outer):
    return jnp.where(s[PAR] == 1, outer.astype(jnp.int32), s[E1]) == 1


def first_kernel(idx_ref, valid_hbm, embed_ref, first_ref, rows_ref, valid_ref, sems):
    near = idx_ref[0] % 2
    rows = pltpu.make_async_copy(embed_ref.at[pl.ds(at(near), HALF), :], rows_ref, sems.at[0])
    flags = pltpu.make_async_copy(valid_hbm, valid_ref, sems.at[1])
    rows.start()
    flags.start()
    flags.wait()
    place = iota(valid_ref.shape, 0) // (valid_ref.shape[0] // 2)
    real = jnp.sum(jnp.where(place == near, valid_ref[...], 0).astype(jnp.float32))
    rows.wait()
    first_ref[...] = marked(normalized(rows_ref[...]), real.astype(jnp.int32))


def normalize_kernel(
    idx_ref, pairs_hbm, count_ref, valid_hbm, embed_ref, s, x_ref, second_ref,
    rows_ref, valid_ref, pairs_ref, sems
):
    small = [(pairs_hbm, pairs_ref), (valid_hbm, valid_ref)]
    small = [pltpu.make_async_copy(a, b, sems.at[4 + p]) for p, (a, b) in enumerate(small)]
    copies = [
        pltpu.make_async_copy(
            embed_ref.at[pl.ds(p * HALF, HALF), :],
            rows_ref.at[pl.ds(p * HALF, HALF), :],
            sems.at[p],
        )
        for p in range(4)
    ]
    for copy in small + copies:
        copy.start()
    for copy in small:
        copy.wait()
    idx = idx_ref[0]
    counts = [jnp.int32(0), jnp.int32(0)]
    for slot in range(pairs_ref.shape[1]):
        live = slot < count_ref[0]
        for b in range(2):
            hit = jnp.logical_and(live, pairs_ref[0, slot] == idx * 2 + b)
            counts[b] = counts[b] + hit.astype(jnp.int32)
    per = valid_ref.shape[0] // 2
    reals = [
        jnp.sum(valid_ref[b * per : (b + 1) * per, :].astype(jnp.float32)).astype(jnp.int32)
        for b in range(2)
    ]
    links = [(c >= 2).astype(jnp.int32) for c in counts]
    s[IDX] = idx
    s[PAR] = idx % 2
    for b in range(2):
        s[V0 + b] = reals[b]
        s[E0 + b] = links[b]
        s[C0 + b] = counts[b]
    lane = iota((TILE, x_ref.shape[1]), 1)
    flags = jnp.where(
        lane == 0,
        links[0].astype(jnp.float32),
        jnp.where(lane == 1, links[1].astype(jnp.float32), 0.0),
    )
    x_ref[2 * BLOCK :, :] = flags.astype(jnp.bfloat16)
    for p, copy in enumerate(copies):
        copy.wait()
        rows = slice(p * HALF, (p + 1) * HALF)
        count = reals[p // 2] - (p % 2) * HALF
        x_ref[rows, :] = marked(normalized(rows_ref[rows, :]), count)
    apart = jnp.logical_and(idx % 2 == 1, links[1] == 0)
    rows = x_ref[pl.ds(at(idx % 2) + HALF, HALF), :].astype(jnp.float32)
    mark = jnp.where(iota(rows.shape, 1) == 0, 2.0 * MARK, 0.0)
    second_ref[...] = jnp.where(apart, mark, rows).astype(jnp.bfloat16)


def own_kernel(s, x_ref, dens_ref, acc_ref):
    for b in range(2):
        rows = x_ref[b * BLOCK : (b + 1) * BLOCK, :]
        dens, sums = terms(rows, rows, s[V0 + b])
        dens_ref[b * BLOCK : (b + 1) * BLOCK, :] = dens
        acc_ref[b * BLOCK : (b + 1) * BLOCK, :] = sums

    @pl.when(s[E0] == 1)
    def _():
        for b in range(2):
            other = x_ref[(1 - b) * BLOCK : (2 - b) * BLOCK, :]
            add_terms(x_ref, (b * BLOCK,), [(other, s[V0 + 1 - b])], dens_ref, acc_ref)


def add_sibling(s, start, use, x_ref, sib_ref, dens_ref, acc_ref):
    @pl.when(use)
    def _():
        count = real_rows(sib_ref, start, BLOCK)
        rights = [(sib_ref[pl.ds(start, BLOCK), :], count)]
        add_linked(s, at(1 - s[PAR]), at(s[PAR]), x_ref, rights, dens_ref, acc_ref)


def beside_kernel(s, x_ref, sib_ref, dens_in, acc_in, dens_ref, acc_ref):
    inner, outer = sibling_links(s, sib_ref)
    add_sibling(s, at(s[PAR]), joined(s, outer), x_ref, sib_ref, dens_ref, acc_ref)


def not_apart(qb_ref):
    head = qb_ref[0:TILE, 0:LANES].astype(jnp.float32)
    first = jnp.logical_and(iota(head.shape, 0) == 0, iota(head.shape, 1) == 0)
    return jnp.sum(jnp.where(first, head, 0.0)) < 1.5 * MARK


def across(s, qb_ref):
    below = jnp.logical_and(s[IDX] > 0, not_apart(qb_ref))
    return jnp.where(s[PAR] == 1, s[E1], below.astype(jnp.int32)) == 1


def middle_kernel(s, x_ref, sib_ref, qa_ref, dens_in, acc_in, dens_ref, acc_ref):
    inner, outer = sibling_links(s, sib_ref)
    near, far = at(s[PAR]), at(1 - s[PAR])
    use = jnp.logical_and(joined(s, outer), inner)
    add_sibling(s, far, use, x_ref, sib_ref, dens_ref, acc_ref)

    @pl.when(jnp.logical_and(s[PAR] == 1, s[E1] == 1))
    def _():
        rights = [(qa_ref[...], real_rows(qa_ref, 0, HALF))]
        add_linked(s, near, far, x_ref, rights, dens_ref, acc_ref)


def partial_sums(s, half, q_ref, x_ref, sib_ref, out_ref, dens_ref):
    inner, outer = sibling_links(s, sib_ref)
    near, far = at(s[PAR]), at(1 - s[PAR])
    sums_go = jnp.where(s[PAR] == 1, s[C1] == 2, s[C0] == 3)

    @pl.when(sums_go)
    def _():
        left = q_ref[...]
        count = jnp.where(s[PAR] == 1, s[V0], s[V1]) * s[E0]
        dens, sums = terms(left, x_ref[pl.ds(far, BLOCK), :], count)
        use = jnp.logical_and(s[E0] == 1, joined(s, outer))
        count = jnp.where(use, real_rows(sib_ref, near, BLOCK), 0)
        more_dens, more_sums = terms(left, sib_ref[pl.ds(near, BLOCK), :], count)
        dens_ref[...] = dens + more_dens
        out_ref[0:HALF, :] = (sums + more_sums).astype(jnp.bfloat16)

    @pl.when(jnp.logical_not(sums_go))
    def _():
        dens_ref[...] = jnp.zeros_like(dens_ref)
        keep = jnp.logical_and(s[E0] == 1, jnp.logical_or(s[PAR] == 0, s[E1] == 1))
        rows = x_ref[pl.ds(far + half * HALF, HALF), :].astype(jnp.float32)
        out_ref[0:HALF, :] = marked(rows, jnp.where(keep, BLOCK, 0))


def along_lanes(dens):
    return jnp.sum(dens.T, axis=0, keepdims=True)


def third_kernel(s, q_ref, x_ref, sib_ref, out_ref, dens_ref):
    partial_sums(s, 0, q_ref, x_ref, sib_ref, out_ref, dens_ref)


def fourth_kernel(s, q_ref, x_ref, sib_ref, dens_a_ref, out_ref, dens_ref):
    partial_sums(s, 1, q_ref, x_ref, sib_ref, out_ref, dens_ref)
    width = out_ref.shape[1]
    both = [along_lanes(dens_a_ref[...]), along_lanes(dens_ref[...])]
    row = jnp.concatenate(both + [jnp.zeros((1, width - BLOCK), jnp.float32)], axis=1)
    place = iota((TILE, width), 0)
    tile = jnp.zeros((TILE, width), jnp.float32)
    for piece in range(3):
        rounded = row.astype(jnp.bfloat16).astype(jnp.float32)
        tile = jnp.where(place == piece, rounded, tile)
        row = row - rounded
    out_ref[HALF:, :] = tile.astype(jnp.bfloat16)


def outer_kernel(s, x_ref, qa_ref, qb_ref, dens_in, acc_in, dens_ref, acc_ref):
    near, far = at(s[PAR]), at(1 - s[PAR])
    linked = across(s, qb_ref)
    rights = [(ref[...], real_rows(ref, 0, HALF)) for ref in (qa_ref, qb_ref)]

    @pl.when(jnp.logical_and(linked, s[PAR] == 0))
    def _():
        add_linked(s, near, far, x_ref, rights, dens_ref, acc_ref)

    @pl.when(jnp.logical_and(linked, jnp.logical_and(s[PAR] == 1, rights[1][1] > 0)))
    def _():
        add_linked(s, near, far, x_ref, rights[1:], dens_ref, acc_ref)


def forward_kernel(s, x_ref, sib_ref, fa_ref, fb_ref, dens_in, acc_in, dens_ref, acc_ref):
    far = at(1 - s[PAR])
    inner, outer = sibling_links(s, sib_ref)
    below = jnp.logical_and(s[IDX] > 1, not_apart(fb_ref))
    beyond = jnp.where(s[PAR] == 1, below.astype(jnp.int32), outer.astype(jnp.int32)) == 1

    @pl.when(jnp.logical_and(jnp.logical_and(joined(s, outer), inner), beyond))
    def _():
        rights = [(ref[...], real_rows(ref, 0, HALF)) for ref in (fa_ref, fb_ref)]
        add_terms(x_ref, (far,), rights, dens_ref, acc_ref)


def what_came(s, qb_ref):
    linked = across(s, qb_ref)
    upper, lone = s[PAR] == 1, s[E0] == 0
    sums = jnp.where(upper, s[C1] == 4, jnp.logical_and(linked, lone))
    rows = jnp.where(upper, s[C1] == 3, jnp.logical_and(linked, jnp.logical_not(lone)))
    return sums, rows


def logs_of(density, real):
    use = iota(density.shape, 1) < real
    return jnp.where(use, jnp.log(jnp.where(use, density, 1.0)), 0.0)


def put_logs(log_ref, block, logs):
    per = BLOCK // LANES
    for part in range(per):
        log_ref[pl.ds(block * per + part, 1), :] = logs[:, part * LANES : (part + 1) * LANES]


def finished(sums, start, real):
    return jnp.where(iota(sums.shape, 0) + start < real, sums, 0.0).astype(jnp.bfloat16)


def far_kernel(
    s, x_ref, qb_ref, q_ref, dens_in, acc_in, log_ref, out_ref, dens_ref, acc_ref, rows_ref, sems
):
    near, far = at(s[PAR]), at(1 - s[PAR])
    sums_came, rows_came = what_came(s, qb_ref)

    @pl.when(rows_came)
    def _():
        count = real_rows(q_ref, 0, HALF)
        add_linked(s, near, far, x_ref, [(q_ref[...], count)], dens_ref, acc_ref)

    @pl.when(jnp.logical_not(rows_came))
    def _():
        @pl.when(sums_came)
        def _():
            acc_ref[pl.ds(near, HALF), :] += q_ref[...].astype(jnp.float32)

        copies = []
        for b in range(2):
            rows = pl.ds(b * BLOCK, BLOCK)
            rows_ref[rows, :] = finished(acc_ref[rows, :], 0, s[V0 + b])
            copy = pltpu.make_async_copy(rows_ref.at[rows, :], out_ref.at[rows, :], sems.at[b])
            copy.start()
            copies.append(copy)
        for b in range(2):
            density = along_lanes(dens_ref[b * BLOCK : (b + 1) * BLOCK, :])
            put_logs(log_ref, b, logs_of(density, s[V0 + b]))
        for copy in copies:
            copy.wait()


def last_kernel(
    s, x_ref, qb_ref, q_ref, dens_ref, acc_ref, log_in, out_in, log_ref, out_ref,
    rows_ref, place_ref, sems
):
    sums_came, rows_came = what_came(s, qb_ref)
    log_copy = pltpu.make_async_copy(place_ref, log_ref, sems.at[4])

    @pl.when(rows_came)
    def _():
        count = real_rows(q_ref, 0, HALF)
        right = q_ref[0:HALF, :]
        kerns = []
        for b in range(2):
            left = x_ref[b * BLOCK : (b + 1) * BLOCK, :]
            kerns.append(kernel_tile(left, right, jnp.where(s[PAR] == b, count, count * s[E0])))
        copies = []
        for b in range(2):
            for half in range(2):
                rows = pl.ds(b * BLOCK + half * HALF, HALF)
                kern = kerns[b][half * HALF : (half + 1) * HALF].astype(jnp.bfloat16)
                sums = acc_ref[rows, :] + jnp.dot(kern, right, preferred_element_type=jnp.float32)
                rows_ref[rows, :] = finished(sums, half * HALF, s[V0 + b])
                copy = pltpu.make_async_copy(
                    rows_ref.at[rows, :], out_ref.at[rows, :], sems.at[2 * b + half]
                )
                copy.start()
                copies.append(copy)
            if b == 0:
                for c in range(2):
                    density = dens_ref[c * BLOCK : (c + 1) * BLOCK, :] + folded(kerns[c])
                    put_logs(place_ref, c, logs_of(along_lanes(density), s[V0 + c]))
                log_copy.start()
                copies.append(log_copy)
        for copy in copies:
            copy.wait()

    @pl.when(jnp.logical_not(rows_came))
    def _():
        place_ref[...] = log_in[...]

        @pl.when(sums_came)
        def _():
            near = at(s[PAR])
            real = jnp.where(s[PAR] == 1, s[V1], s[V0])
            rows = pl.ds(near + HALF, HALF)
            sums = acc_ref[rows, :] + q_ref[0:HALF, :].astype(jnp.float32)
            rows_ref[rows, :] = finished(sums, HALF, real)
            copy = pltpu.make_async_copy(rows_ref.at[rows, :], out_ref.at[rows, :], sems.at[0])
            copy.start()
            tile = q_ref[HALF:, :].astype(jnp.float32)
            came = jnp.sum(jnp.where(iota(tile.shape, 0) < 3, tile, 0.0), axis=0, keepdims=True)
            density = along_lanes(dens_ref[pl.ds(near, BLOCK), :]) + came[:, 0:BLOCK]
            put_logs(place_ref, s[PAR], logs_of(density, real))
            log_copy.start()
            copy.wait()
            log_copy.wait()

        @pl.when(jnp.logical_not(sums_came))
        def _():
            log_copy.start()
            log_copy.wait()


def call(kernel, us, in_spaces, operands, outs, out_spaces="", aliases=None, scratch=()):
    spaces = {"s": SM, "v": VM, "h": HB}
    out_spaces = out_spaces or "v" * len(outs)
    return pl.pallas_call(
        kernel,
        in_specs=[spaces[c] for c in in_spaces],
        out_specs=[spaces[c] for c in out_spaces],
        out_shape=outs,
        input_output_aliases=aliases or {},
        scratch_shapes=list(scratch),
        compiler_params=pltpu.CompilerParams(vmem_limit_bytes=16 << 20),
        cost_estimate=pl.CostEstimate(flops=int(us * 1.15e9), bytes_accessed=1 << 10, transcendentals=0),
    )(
        *[
            pltpu.with_memory_space_constraint(x, pltpu.HBM) if c == "h" else x
            for c, x in zip(in_spaces, operands)
        ]
    )


def after(value, *others):
    return lax.optimization_barrier((value, *others))[0]


def per_device(embed, valid, pairs, pair_count):
    width = embed.shape[1]
    chips = lax.axis_size("cluster") // 2
    idx = lax.axis_index("cluster").astype(jnp.int32).reshape(1)
    inchip = [(2 * c + k, 2 * c + 1 - k) for c in range(chips) for k in range(2)]
    edges = [(2 * c + 1, 2 * c + 2) for c in range(chips - 1)]
    edges = edges + [(b, a) for a, b in edges]

    def over_edge(block):
        return lax.ppermute(block, "cluster", edges)

    def to_sibling(block):
        return lax.ppermute(block, "cluster", inchip)

    bf16 = lambda rows: jax.ShapeDtypeStruct((rows, width), jnp.bfloat16)
    f32 = lambda rows, cols: jax.ShapeDtypeStruct((rows, cols), jnp.float32)
    state = [f32(2 * BLOCK, LANES), f32(2 * BLOCK, width)]
    dma = lambda count: pltpu.SemaphoreType.DMA((count,))
    vmem = lambda rows: pltpu.VMEM((rows, width), jnp.bfloat16)

    flags = valid.reshape(-1, LANES)
    (first,) = call(
        first_kernel,
        6.0,
        "shh",
        (idx, flags, embed),
        [bf16(HALF)],
        scratch=(vmem(HALF), pltpu.VMEM(flags.shape, jnp.int32), dma(2)),
    )
    qa = over_edge(first)
    table, x, second = call(
        normalize_kernel,
        14.0,
        "shshh",
        (after(idx, first), pairs.T, pair_count, flags, embed),
        [jax.ShapeDtypeStruct((8,), jnp.int32), bf16(2 * BLOCK + TILE), bf16(HALF)],
        "svv",
        scratch=(
            vmem(2 * BLOCK),
            pltpu.VMEM(flags.shape, jnp.int32),
            pltpu.SMEM(pairs.shape[::-1], jnp.int32),
            dma(6),
        ),
    )
    qb = over_edge(second)
    sib = to_sibling(x)
    dens, acc = call(own_kernel, 60, "sv", (table, x), state)
    dens, acc = call(
        beside_kernel, 13.0, "svvvv", (table, x, sib, dens, acc), state, aliases={3: 0, 4: 1}
    )
    third, dens_a = call(
        third_kernel,
        10.0,
        "svvv",
        (table, qa, after(x, acc), sib),
        [bf16(HALF), f32(HALF, LANES)],
    )
    qc = over_edge(third)
    dens, acc, _ = lax.optimization_barrier((dens, acc, third))
    dens, acc = call(
        middle_kernel, 15.0, "svvvvv", (table, x, sib, qa, dens, acc), state, aliases={4: 0, 5: 1}
    )
    fourth, _ = call(
        fourth_kernel,
        10.0,
        "svvvv",
        (table, qb, after(x, acc), sib, dens_a),
        [bf16(HALF + TILE), f32(HALF, LANES)],
    )
    dens, acc, fourth = lax.optimization_barrier((dens, acc, fourth))
    qd = over_edge(fourth)
    fa = to_sibling(after(qa, fourth))
    fb = to_sibling(after(qb, fourth))
    dens, acc = call(
        outer_kernel, 15.0, "svvvvv", (table, x, qa, qb, dens, acc), state, aliases={4: 0, 5: 1}
    )
    dens, acc = call(
        forward_kernel,
        15.0,
        "svvvvvv",
        (table, x, sib, fa, fb, dens, acc),
        state,
        aliases={5: 0, 6: 1},
    )
    logs, sums, dens, acc = call(
        far_kernel,
        5.0,
        "svvvvv",
        (table, x, qb, qc, dens, acc),
        [f32(2 * BLOCK // LANES, LANES), bf16(2 * BLOCK)] + state,
        "vhvv",
        aliases={4: 2, 5: 3},
        scratch=(vmem(2 * BLOCK), dma(2)),
    )
    logs, sums = call(
        last_kernel,
        5.0,
        "svvvvvvh",
        (table, x, qb, qd, dens, acc, logs, sums),
        [f32(2 * BLOCK // LANES, LANES), bf16(2 * BLOCK)],
        "hh",
        aliases={7: 1},
        scratch=(
            vmem(2 * BLOCK),
            pltpu.VMEM((2 * BLOCK // LANES, LANES), jnp.float32),
            dma(5),
        ),
    )
    return logs.reshape(-1), sums


def solution(mesh):
    both = ("groups", "cluster")
    return jax.shard_map(
        per_device,
        mesh=mesh,
        in_specs=(P(both, None), P(both), P(both, None), P(both)),
        out_specs=(P(both), P(both, None)),
        check_vma=False,
    )
```

profile of v0, /device:TPU:17, one launch (start us, length us, event | category | flops | bytes accessed | tf_op | source)
XLA Modules:
  0.0 45.2 jit_solution(8894089714019753019)
XLA Ops:
  0.6 1.2 %shard_map.59 = bf16[256,768]{1,0:T(8,128)(2,1)S(1)} custom-call(s32[1]{0:T(128)} %bitcast.idx_ref, s32[8,128]{1,0:T(8,128)} %bitcast.4, bf16[1024,768]{1,0:T(8,128)(2,1)} %embed_ref.3), custom_call_target="tpu_custom_call" | custom-call | flops 6899999744 | bytes 1024 | tf_op jit(solution)/shard_map/pallas_call | solution.py:418
  1.8 3.7 %collective-permute-start.2 = (bf16[256,768]{1,0:T(8,128)(2,1)S(1)}, bf16[256,768]{1,0:T(8,128)(2,1)S(1)}, u32[]{:S(2)}, u32[]{:S(2)}) collective-permute-start(bf16[256,768]{1,0:T(8,128)(2,1)S(1)} %shard_map.59), channel_id=1, source_target_pairs={{1,2},{3,4},{5,6},{7,8},{9,10},{11,12},{13,14},{2,1},{4,3},{6,5},{... | collective-permute-start | bytes 1179656 | tf_op jit(solution)/shard_map/ppermute | solution.py:448
  6.2 2.2 %shard_map.60 = (s32[8]{0:T(128)S(1)}, bf16[1040,768]{1,0:T(8,128)(2,1)S(1)}, bf16[256,768]{1,0:T(8,128)(2,1)S(1)}) custom-call(s32[1]{0:T(128)} %bitcast.idx_ref, s32[2,7]{1,0:T(2,128)} %bitcast.6, s32[1]{0:T(128)S(6)} %copy.28.count_ref, s32[8,128]{1,0:T(8,128)} %bitcast.5, bf16[1024,768]{1,0:T(8,128)(2,1)} %embed_ref.3), custom_call_target="tpu_custom_call" | custom-call | flops 16099999744 | bytes 1024 | tf_op jit(solution)/shard_map/pallas_call | solution.py:418
  8.4 1.9 %collective-permute-start = (bf16[256,768]{1,0:T(8,128)(2,1)S(1)}, bf16[256,768]{1,0:T(8,128)(2,1)S(1)}, u32[]{:S(2)}, u32[]{:S(2)}) collective-permute-start(bf16[256,768]{1,0:T(8,128)(2,1)S(1)} %get-tuple-element.37), channel_id=1, source_target_pairs={{1,2},{3,4},{5,6},{7,8},{9,10},{11,12},{13,14},{2,1},{4,3},{6,5},{... | collective-permute-start | bytes 1179656 | tf_op jit(solution)/shard_map/ppermute | solution.py:448
  10.3 1.6 %collective-permute-start.1 = (bf16[1040,768]{1,0:T(8,128)(2,1)S(1)}, bf16[1040,768]{1,0:T(8,128)(2,1)S(1)}, u32[]{:S(2)}, u32[]{:S(2)}) collective-permute-start(bf16[1040,768]{1,0:T(8,128)(2,1)S(1)} %get-tuple-element.48.x_ref), channel_id=1, source_target_pairs={{0,1},{1,0},{2,3},{3,2},{4,5},{5,4},{6,7},{7,6},{8,9},{9,8},{10,11... | collective-permute-start | bytes 4792328 | tf_op jit(solution)/shard_map/ppermute | solution.py:451
  11.9 2.6 %shard_map.61 = (f32[1024,128]{1,0:T(8,128)S(1)}, f32[1024,768]{1,0:T(8,128)S(1)}) custom-call(s32[8]{0:T(128)S(1)} %get-tuple-element.35.s, bf16[1040,768]{1,0:T(8,128)(2,1)S(1)} %get-tuple-element.48.x_ref), custom_call_target="tpu_custom_call" | custom-call | flops 69000003584 | bytes 1024 | tf_op jit(solution)/shard_map/pallas_call | solution.py:418
  14.5 0.5 %collective-permute-done.1.sib_ref = bf16[1040,768]{1,0:T(8,128)(2,1)S(1)} collective-permute-done((bf16[1040,768]{1,0:T(8,128)(2,1)S(1)}, bf16[1040,768]{1,0:T(8,128)(2,1)S(1)}, u32[]{:S(2)}, u32[]{:S(2)}) %collective-permute-start.1) | collective-permute-done | bytes 1597472 | tf_op jit(solution)/shard_map/ppermute | solution.py:451
  15.0 2.0 %shard_map.62 = (f32[1024,128]{1,0:T(8,128)S(1)}, f32[1024,768]{1,0:T(8,128)S(1)}) custom-call(s32[8]{0:T(128)S(1)} %get-tuple-element.35.s, bf16[1040,768]{1,0:T(8,128)(2,1)S(1)} %get-tuple-element.48.x_ref, bf16[1040,768]{1,0:T(8,128)(2,1)S(1)} %collective-permute-done.1.sib_ref, ...), custom_call_target="tpu_custom_call", output_to_operand_aliasing={{0}: (3, {}), {1}: (4, {})} | custom-call | flops 14949999616 | bytes 1024 | tf_op jit(solution)/shard_map/pallas_call | solution.py:418
  17.1 2.4 %collective-permute-done.2.q_ref.qa_ref = bf16[256,768]{1,0:T(8,128)(2,1)S(1)} collective-permute-done((bf16[256,768]{1,0:T(8,128)(2,1)S(1)}, bf16[256,768]{1,0:T(8,128)(2,1)S(1)}, u32[]{:S(2)}, u32[]{:S(2)}) %collective-permute-start.2) | collective-permute-done | bytes 393248 | tf_op jit(solution)/shard_map/ppermute | solution.py:448
  19.4 2.0 %shard_map.63 = (bf16[256,768]{1,0:T(8,128)(2,1)S(1)}, f32[256,128]{1,0:T(8,128)S(1)}) custom-call(s32[8]{0:T(128)S(1)} %get-tuple-element.35.s, bf16[256,768]{1,0:T(8,128)(2,1)S(1)} %collective-permute-done.2.q_ref.qa_ref, bf16[1040,768]{1,0:T(8,128)(2,1)S(1)} %get-tuple-element.48.x_ref, bf16[1040,768]{1,0:T(8,128)(2,1)S(1)} %collective-permute-done.1.sib_ref), custom_call_target="tpu_custom_call" | custom-call | flops 11500000256 | bytes 1024 | tf_op jit(solution)/shard_map/pallas_call | solution.py:418
  21.4 2.4 %collective-permute-start.4 = (bf16[256,768]{1,0:T(8,128)(2,1)S(1)}, bf16[256,768]{1,0:T(8,128)(2,1)S(1)}, u32[]{:S(2)}, u32[]{:S(2)}) collective-permute-start(bf16[256,768]{1,0:T(8,128)(2,1)S(1)} %get-tuple-element.43), channel_id=1, source_target_pairs={{1,2},{3,4},{5,6},{7,8},{9,10},{11,12},{13,14},{2,1},{4,3},{6,5},{... | collective-permute-start | bytes 1179656 | tf_op jit(solution)/shard_map/ppermute | solution.py:448
  23.8 3.4 %shard_map.64 = (f32[1024,128]{1,0:T(8,128)S(1)}, f32[1024,768]{1,0:T(8,128)S(1)}) custom-call(s32[8]{0:T(128)S(1)} %get-tuple-element.35.s, bf16[1040,768]{1,0:T(8,128)(2,1)S(1)} %get-tuple-element.48.x_ref, bf16[1040,768]{1,0:T(8,128)(2,1)S(1)} %collective-permute-done.1.sib_ref, ...), custom_call_target="tpu_custom_call", output_to_operand_aliasing={{0}: (4, {}), {1}: (5, {})} | custom-call | flops 17250000896 | bytes 1024 | tf_op jit(solution)/shard_map/pallas_call | solution.py:418
  27.2 0.0 collective-permute-done.q_ref.qb_ref
  27.2 2.7 %shard_map.65 = (bf16[272,768]{1,0:T(8,128)(2,1)S(1)}, f32[256,128]{1,0:T(8,128)}) custom-call(s32[8]{0:T(128)S(1)} %get-tuple-element.35.s, bf16[256,768]{1,0:T(8,128)(2,1)S(1)} %collective-permute-done.q_ref.qb_ref, bf16[1040,768]{1,0:T(8,128)(2,1)S(1)} %get-tuple-element.48.x_ref, bf16[1040,768]{1,0:T(8,128)(2,1)S(1)} %collective-permute-done.1.sib_ref, ...), custom_call_target="tpu_custom_call" | custom-call | flops 11500000256 | bytes 1024 | tf_op jit(solution)/shard_map/pallas_call | solution.py:418
  29.9 1.9 %collective-permute-start.3 = (bf16[272,768]{1,0:T(8,128)(2,1)S(1)}, bf16[272,768]{1,0:T(8,128)(2,1)S(1)}, u32[]{:S(2)}, u32[]{:S(2)}) collective-permute-start(bf16[272,768]{1,0:T(8,128)(2,1)S(1)} %get-tuple-element.51), channel_id=1, source_target_pairs={{1,2},{3,4},{5,6},{7,8},{9,10},{11,12},{13,14},{2,1},{4,3},{6,5},{... | collective-permute-start | bytes 1253384 | tf_op jit(solution)/shard_map/ppermute | solution.py:448
  31.8 0.1 collective-permute-start.5
  31.9 0.5 %collective-permute-start.6 = (bf16[256,768]{1,0:T(8,128)(2,1)S(1)}, bf16[256,768]{1,0:T(8,128)(2,1)S(1)}, u32[]{:S(2)}, u32[]{:S(2)}) collective-permute-start(bf16[256,768]{1,0:T(8,128)(2,1)S(1)} %collective-permute-done.q_ref.qb_ref), channel_id=1, source_target_pairs={{0,1},{1,0},{2,3},{3,2},{4,5},{5,4},{6,7},{7,6},{8,9},{9,8},{10,11... | collective-permute-start | bytes 1179656 | tf_op jit(solution)/shard_map/ppermute | solution.py:451
  32.4 1.7 %shard_map.66 = (f32[1024,128]{1,0:T(8,128)S(1)}, f32[1024,768]{1,0:T(8,128)S(1)}) custom-call(s32[8]{0:T(128)S(1)} %get-tuple-element.35.s, bf16[1040,768]{1,0:T(8,128)(2,1)S(1)} %get-tuple-element.48.x_ref, bf16[256,768]{1,0:T(8,128)(2,1)S(1)} %collective-permute-done.2.q_ref.qa_ref, ...), custom_call_target="tpu_custom_call", output_to_operand_aliasing={{0}: (4, {}), {1}: (5, {})} | custom-call | flops 17250000896 | bytes 1024 | tf_op jit(solution)/shard_map/pallas_call | solution.py:418
  34.1 0.0 collective-permute-done.6.fb_ref
  34.2 0.7 %shard_map.67 = (f32[1024,128]{1,0:T(8,128)S(1)}, f32[1024,768]{1,0:T(8,128)S(1)}) custom-call(s32[8]{0:T(128)S(1)} %get-tuple-element.35.s, bf16[1040,768]{1,0:T(8,128)(2,1)S(1)} %get-tuple-element.48.x_ref, bf16[1040,768]{1,0:T(8,128)(2,1)S(1)} %collective-permute-done.1.sib_ref, ...), custom_call_target="tpu_custom_call", output_to_operand_aliasing={{0}: (5, {}), {1}: (6, {})} | custom-call | flops 17250000896 | bytes 1024 | tf_op jit(solution)/shard_map/pallas_call | solution.py:418
  34.8 4.4 %collective-permute-done.4.q_ref = bf16[256,768]{1,0:T(8,128)(2,1)S(1)} collective-permute-done((bf16[256,768]{1,0:T(8,128)(2,1)S(1)}, bf16[256,768]{1,0:T(8,128)(2,1)S(1)}, u32[]{:S(2)}, u32[]{:S(2)}) %collective-permute-start.4) | collective-permute-done | bytes 393248 | tf_op jit(solution)/shard_map/ppermute | solution.py:448
  39.2 2.2 %shard_map.68 = (f32[8,128]{1,0:T(8,128)S(1)}, bf16[1024,768]{1,0:T(8,128)(2,1)}, f32[1024,128]{1,0:T(8,128)S(1)}, f32[1024,768]{1,0:T(8,128)S(1)}) custom-call(s32[8]{0:T(128)S(1)} %get-tuple-element.35.s, bf16[1040,768]{1,0:T(8,128)(2,1)S(1)} %get-tuple-element.48.x_ref, ...), custom_call_target="tpu_custom_call", output_to_operand_aliasing={{2}: (4, {}), {3}: (5, {})} | custom-call | flops 5750000128 | bytes 1024 | tf_op jit(solution)/shard_map/pallas_call | solution.py:418
  41.4 2.3 %collective-permute-done.3.q_ref = bf16[272,768]{1,0:T(8,128)(2,1)S(1)} collective-permute-done((bf16[272,768]{1,0:T(8,128)(2,1)S(1)}, bf16[272,768]{1,0:T(8,128)(2,1)S(1)}, u32[]{:S(2)}, u32[]{:S(2)}) %collective-permute-start.3) | collective-permute-done | bytes 417824 | tf_op jit(solution)/shard_map/ppermute | solution.py:448
  43.7 1.3 %shard_map.69 = (f32[8,128]{1,0:T(8,128)}, bf16[1024,768]{1,0:T(8,128)(2,1)}) custom-call(s32[8]{0:T(128)S(1)} %get-tuple-element.35.s, bf16[1040,768]{1,0:T(8,128)(2,1)S(1)} %get-tuple-element.48.x_ref, bf16[256,768]{1,0:T(8,128)(2,1)S(1)} %collective-permute-done.q_ref.qb_ref, ...), custom_call_target="tpu_custom_call", output_to_operand_aliasing={{1}: (7, {})} | custom-call | flops 5750000128 | bytes 1024 | tf_op jit(solution)/shard_map/pallas_call | solution.py:418
  (1 shorter events, 0.0 us)
Async XLA Ops:
  1.8 17.6 %collective-permute-start.2 = (bf16[256,768]{1,0:T(8,128)(2,1)S(1)}, bf16[256,768]{1,0:T(8,128)(2,1)S(1)}, u32[]{:S(2)}, u32[]{:S(2)}) collective-permute-start(bf16[256,768]{1,0:T(8,128)(2,1)S(1)} %shard_map.59), channel_id=1, source_target_pairs={{1,2},{3,4},{5,6},{7,8},{9,10},{11,12},{13,14},{2,1},{4,3},{6,5},{... | collective-permute-start | bytes 1179656 | tf_op jit(solution)/shard_map/ppermute | solution.py:448
  8.4 18.8 %collective-permute-start = (bf16[256,768]{1,0:T(8,128)(2,1)S(1)}, bf16[256,768]{1,0:T(8,128)(2,1)S(1)}, u32[]{:S(2)}, u32[]{:S(2)}) collective-permute-start(bf16[256,768]{1,0:T(8,128)(2,1)S(1)} %get-tuple-element.37), channel_id=1, source_target_pairs={{1,2},{3,4},{5,6},{7,8},{9,10},{11,12},{13,14},{2,1},{4,3},{6,5},{... | collective-permute-start | bytes 1179656 | tf_op jit(solution)/shard_map/ppermute | solution.py:448
  10.3 4.6 %collective-permute-start.1 = (bf16[1040,768]{1,0:T(8,128)(2,1)S(1)}, bf16[1040,768]{1,0:T(8,128)(2,1)S(1)}, u32[]{:S(2)}, u32[]{:S(2)}) collective-permute-start(bf16[1040,768]{1,0:T(8,128)(2,1)S(1)} %get-tuple-element.48.x_ref), channel_id=1, source_target_pairs={{0,1},{1,0},{2,3},{3,2},{4,5},{5,4},{6,7},{7,6},{8,9},{9,8},{10,11... | collective-permute-start | bytes 4792328 | tf_op jit(solution)/shard_map/ppermute | solution.py:451
  21.4 17.8 %collective-permute-start.4 = (bf16[256,768]{1,0:T(8,128)(2,1)S(1)}, bf16[256,768]{1,0:T(8,128)(2,1)S(1)}, u32[]{:S(2)}, u32[]{:S(2)}) collective-permute-start(bf16[256,768]{1,0:T(8,128)(2,1)S(1)} %get-tuple-element.43), channel_id=1, source_target_pairs={{1,2},{3,4},{5,6},{7,8},{9,10},{11,12},{13,14},{2,1},{4,3},{6,5},{... | collective-permute-start | bytes 1179656 | tf_op jit(solution)/shard_map/ppermute | solution.py:448
  29.9 13.8 %collective-permute-start.3 = (bf16[272,768]{1,0:T(8,128)(2,1)S(1)}, bf16[272,768]{1,0:T(8,128)(2,1)S(1)}, u32[]{:S(2)}, u32[]{:S(2)}) collective-permute-start(bf16[272,768]{1,0:T(8,128)(2,1)S(1)} %get-tuple-element.51), channel_id=1, source_target_pairs={{1,2},{3,4},{5,6},{7,8},{9,10},{11,12},{13,14},{2,1},{4,3},{6,5},{... | collective-permute-start | bytes 1253384 | tf_op jit(solution)/shard_map/ppermute | solution.py:448
  31.8 2.3 %collective-permute-start.5 = (bf16[256,768]{1,0:T(8,128)(2,1)S(1)}, bf16[256,768]{1,0:T(8,128)(2,1)S(1)}, u32[]{:S(2)}, u32[]{:S(2)}) collective-permute-start(bf16[256,768]{1,0:T(8,128)(2,1)S(1)} %collective-permute-done.2.q_ref.qa_ref), channel_id=1, source_target_pairs={{0,1},{1,0},{2,3},{3,2},{4,5},{5,4},{6,7},{7,6},{8,9},{9,8},{10,11... | collective-permute-start | bytes 1179656 | tf_op jit(solution)/shard_map/ppermute | solution.py:451
  31.9 2.3 %collective-permute-start.6 = (bf16[256,768]{1,0:T(8,128)(2,1)S(1)}, bf16[256,768]{1,0:T(8,128)(2,1)S(1)}, u32[]{:S(2)}, u32[]{:S(2)}) collective-permute-start(bf16[256,768]{1,0:T(8,128)(2,1)S(1)} %collective-permute-done.q_ref.qb_ref), channel_id=1, source_target_pairs={{0,1},{1,0},{2,3},{3,2},{4,5},{5,4},{6,7},{7,6},{8,9},{9,8},{10,11... | collective-permute-start | bytes 1179656 | tf_op jit(solution)/shard_map/ppermute | solution.py:451
where the time goes:
time: 45 us; the launch traced here: 45.2 us
  Pallas kernels  21.9 us (49%)
  starting transfers between devices  12.1 us (27%)
  waiting for transfers between devices  9.57 us (21%)
  between operations  1.57 us (3%)
    pallas_call x11, Pallas kernels, call(): pl.pallas_call(kernel, in_specs=[spaces[c] for c in in_spaces], out_specs...  21.9 us
    ppermute x4, starting transfers between devices, over_edge(): return lax.ppermute(block, 'cluster', edges)  9.93 us
    ppermute x4, waiting for transfers between devices, over_edge(): return lax.ppermute(block, 'cluster', edges)  9.06 us
    ppermute x3, starting transfers between devices, to_sibling(): return lax.ppermute(block, 'cluster', inchip)  2.14 us
  transfers between devices with their start and end apart: 7, of which 4 were waited for; matrix products, arithmetic and copies ran while one was open for 0% of the time, Pallas kernels for 43%

commit v1 on v0

--- a/solution.py
+++ b/solution.py
@@ -195,7 +195,12 @@
         add_linked(s, at(1 - s[PAR]), at(s[PAR]), x_ref, rights, dens_ref, acc_ref)
 
 
-def beside_kernel(s, x_ref, sib_ref, dens_in, acc_in, dens_ref, acc_ref):
+def beside_kernel(s, x_ref, sib_ref, dens_in, acc_in, third_ref, fourth_ref, dens_ref, acc_ref):
+    far = at(1 - s[PAR])
+    keep = jnp.logical_and(s[E0] == 1, jnp.logical_or(s[PAR] == 0, s[E1] == 1))
+    for half, ref in enumerate((third_ref, fourth_ref)):
+        rows = x_ref[pl.ds(far + half * HALF, HALF), :].astype(jnp.float32)
+        ref[0:HALF, :] = marked(rows, jnp.where(keep, BLOCK, 0))
     inner, outer = sibling_links(s, sib_ref)
     add_sibling(s, at(s[PAR]), joined(s, outer), x_ref, sib_ref, dens_ref, acc_ref)
 
@@ -223,55 +228,61 @@
         add_linked(s, near, far, x_ref, rights, dens_ref, acc_ref)
 
 
-def partial_sums(s, half, q_ref, x_ref, sib_ref, out_ref, dens_ref):
-    inner, outer = sibling_links(s, sib_ref)
+def sums_go(s):
+    return jnp.where(s[PAR] == 1, s[C1] == 2, s[C0] == 3)
+
+
+def partial_sums(s, q_ref, x_ref, sib_ref, out_ref, dens_ref):
+    _, outer = sibling_links(s, sib_ref)
     near, far = at(s[PAR]), at(1 - s[PAR])
-    sums_go = jnp.where(s[PAR] == 1, s[C1] == 2, s[C0] == 3)
-
-    @pl.when(sums_go)
-    def _():
-        left = q_ref[...]
-        count = jnp.where(s[PAR] == 1, s[V0], s[V1]) * s[E0]
-        dens, sums = terms(left, x_ref[pl.ds(far, BLOCK), :], count)
-        use = jnp.logical_and(s[E0] == 1, joined(s, outer))
-        count = jnp.where(use, real_rows(sib_ref, near, BLOCK), 0)
-        more_dens, more_sums = terms(left, sib_ref[pl.ds(near, BLOCK), :], count)
-        dens_ref[...] = dens + more_dens
-        out_ref[0:HALF, :] = (sums + more_sums).astype(jnp.bfloat16)
-
-    @pl.when(jnp.logical_not(sums_go))
-    def _():
-        dens_ref[...] = jnp.zeros_like(dens_ref)
-        keep = jnp.logical_and(s[E0] == 1, jnp.logical_or(s[PAR] == 0, s[E1] == 1))
-        rows = x_ref[pl.ds(far + half * HALF, HALF), :].astype(jnp.float32)
-        out_ref[0:HALF, :] = marked(rows, jnp.where(keep, BLOCK, 0))
+    left = q_ref[...]
+    count = jnp.where(s[PAR] == 1, s[V0], s[V1]) * s[E0]
+    use = jnp.logical_and(s[E0] == 1, joined(s, outer))
+    beside = jnp.where(use, real_rows(sib_ref, near, BLOCK), 0)
+    rights = [(x_ref[pl.ds(far, BLOCK), :], count), (sib_ref[pl.ds(near, BLOCK), :], beside)]
+    kerns = [kernel_tile(left, right, count) for right, count in rights]
+    sums = [
+        jnp.dot(kern.astype(jnp.bfloat16), right, preferred_element_type=jnp.float32)
+        for kern, (right, _) in zip(kerns, rights)
+    ]
+    dens_ref[...] = folded(kerns[0]) + folded(kerns[1])
+    out_ref[0:HALF, :] = (sums[0] + sums[1]).astype(jnp.bfloat16)
 
 
 def along_lanes(dens):
     return jnp.sum(dens.T, axis=0, keepdims=True)
 
 
-def third_kernel(s, q_ref, x_ref, sib_ref, out_ref, dens_ref):
-    partial_sums(s, 0, q_ref, x_ref, sib_ref, out_ref, dens_ref)
-
-
-def fourth_kernel(s, q_ref, x_ref, sib_ref, dens_a_ref, out_ref, dens_ref):
-    partial_sums(s, 1, q_ref, x_ref, sib_ref, out_ref, dens_ref)
-    width = out_ref.shape[1]
-    both = [along_lanes(dens_a_ref[...]), along_lanes(dens_ref[...])]
-    row = jnp.concatenate(both + [jnp.zeros((1, width - BLOCK), jnp.float32)], axis=1)
-    place = iota((TILE, width), 0)
-    tile = jnp.zeros((TILE, width), jnp.float32)
-    for piece in range(3):
-        rounded = row.astype(jnp.bfloat16).astype(jnp.float32)
-        tile = jnp.where(place == piece, rounded, tile)
-        row = row - rounded
-    out_ref[HALF:, :] = tile.astype(jnp.bfloat16)
-
-
-def outer_kernel(s, x_ref, qa_ref, qb_ref, dens_in, acc_in, dens_ref, acc_ref):
+def third_kernel(s, q_ref, x_ref, sib_ref, out_in, out_ref, dens_ref):
+    @pl.when(sums_go(s))
+    def _():
+        partial_sums(s, q_ref, x_ref, sib_ref, out_ref, dens_ref)
+
+
+def fourth_kernel(s, q_ref, x_ref, sib_ref, dens_a_ref, out_in, out_ref, dens_ref):
+    @pl.when(sums_go(s))
+    def _():
+        partial_sums(s, q_ref, x_ref, sib_ref, out_ref, dens_ref)
+        width = out_ref.shape[1]
+        both = [along_lanes(dens_a_ref[...]), along_lanes(dens_ref[...])]
+        row = jnp.concatenate(both + [jnp.zeros((1, width - BLOCK), jnp.float32)], axis=1)
+        place = iota((TILE, width), 0)
+        tile = jnp.zeros((TILE, width), jnp.float32)
+        for piece in range(3):
+            rounded = row.astype(jnp.bfloat16).astype(jnp.float32)
+            tile = jnp.where(place == piece, rounded, tile)
+            row = row - rounded
+        out_ref[HALF:, :] = tile.astype(jnp.bfloat16)
+
+
+def outer_kernel(s, x_ref, qa_ref, qb_ref, dens_in, acc_in, came, dens_ref, acc_ref):
     near, far = at(s[PAR]), at(1 - s[PAR])
     linked = across(s, qb_ref)
+    upper, lone = s[PAR] == 1, s[E0] == 0
+    sums = jnp.where(upper, s[C1] == 4, jnp.logical_and(linked, lone))
+    rows = jnp.where(upper, s[C1] == 3, jnp.logical_and(linked, jnp.logical_not(lone)))
+    came[0] = sums.astype(jnp.int32)
+    came[1] = rows.astype(jnp.int32)
     rights = [(ref[...], real_rows(ref, 0, HALF)) for ref in (qa_ref, qb_ref)]
 
     @pl.when(jnp.logical_and(linked, s[PAR] == 0))
@@ -295,14 +306,6 @@
         add_terms(x_ref, (far,), rights, dens_ref, acc_ref)
 
 
-def what_came(s, qb_ref):
-    linked = across(s, qb_ref)
-    upper, lone = s[PAR] == 1, s[E0] == 0
-    sums = jnp.where(upper, s[C1] == 4, jnp.logical_and(linked, lone))
-    rows = jnp.where(upper, s[C1] == 3, jnp.logical_and(linked, jnp.logical_not(lone)))
-    return sums, rows
-
-
 def logs_of(density, real):
     use = iota(density.shape, 1) < real
     return jnp.where(use, jnp.log(jnp.where(use, density, 1.0)), 0.0)
@@ -319,19 +322,19 @@
 
 
 def far_kernel(
-    s, x_ref, qb_ref, q_ref, dens_in, acc_in, log_ref, out_ref, dens_ref, acc_ref, rows_ref, sems
+    s, came, x_ref, q_ref, dens_in, acc_in, log_out, out_ref, dens_ref, acc_ref,
+    rows_ref, log_ref, sems
 ):
     near, far = at(s[PAR]), at(1 - s[PAR])
-    sums_came, rows_came = what_came(s, qb_ref)
-
-    @pl.when(rows_came)
+
+    @pl.when(came[1] == 1)
     def _():
         count = real_rows(q_ref, 0, HALF)
         add_linked(s, near, far, x_ref, [(q_ref[...], count)], dens_ref, acc_ref)
 
-    @pl.when(jnp.logical_not(rows_came))
-    def _():
-        @pl.when(sums_came)
+    @pl.when(came[1] == 0)
+    def _():
+        @pl.when(came[0] == 1)
         def _():
             acc_ref[pl.ds(near, HALF), :] += q_ref[...].astype(jnp.float32)
 
@@ -345,18 +348,19 @@
         for b in range(2):
             density = along_lanes(dens_ref[b * BLOCK : (b + 1) * BLOCK, :])
             put_logs(log_ref, b, logs_of(density, s[V0 + b]))
-        for copy in copies:
+        copy = pltpu.make_async_copy(log_ref, log_out, sems.at[2])
+        copy.start()
+        for copy in copies + [copy]:
             copy.wait()
 
 
 def last_kernel(
-    s, x_ref, qb_ref, q_ref, dens_ref, acc_ref, log_in, out_in, log_ref, out_ref,
-    rows_ref, place_ref, sems
+    s, came, x_ref, q_ref, dens_ref, acc_ref, log_in, out_in, log_out, out_ref,
+    rows_ref, log_ref, sems
 ):
-    sums_came, rows_came = what_came(s, qb_ref)
-    log_copy = pltpu.make_async_copy(place_ref, log_ref, sems.at[4])
-
-    @pl.when(rows_came)
+    log_copy = pltpu.make_async_copy(log_ref, log_out, sems.at[4])
+
+    @pl.when(came[1] == 1)
     def _():
         count = real_rows(q_ref, 0, HALF)
         right = q_ref[0:HALF, :]
@@ -379,37 +383,31 @@
             if b == 0:
                 for c in range(2):
                     density = dens_ref[c * BLOCK : (c + 1) * BLOCK, :] + folded(kerns[c])
-                    put_logs(place_ref, c, logs_of(along_lanes(density), s[V0 + c]))
+                    put_logs(log_ref, c, logs_of(along_lanes(density), s[V0 + c]))
                 log_copy.start()
                 copies.append(log_copy)
         for copy in copies:
             copy.wait()
 
-    @pl.when(jnp.logical_not(rows_came))
-    def _():
-        place_ref[...] = log_in[...]
-
-        @pl.when(sums_came)
-        def _():
-            near = at(s[PAR])
-            real = jnp.where(s[PAR] == 1, s[V1], s[V0])
-            rows = pl.ds(near + HALF, HALF)
-            sums = acc_ref[rows, :] + q_ref[0:HALF, :].astype(jnp.float32)
-            rows_ref[rows, :] = finished(sums, HALF, real)
-            copy = pltpu.make_async_copy(rows_ref.at[rows, :], out_ref.at[rows, :], sems.at[0])
-            copy.start()
+    @pl.when(came[0] == 1)
+    def _():
+        near = at(s[PAR])
+        real = jnp.where(s[PAR] == 1, s[V1], s[V0])
+        rows = pl.ds(near + HALF, HALF)
+        sums = acc_ref[rows, :] + q_ref[0:HALF, :].astype(jnp.float32)
+        rows_ref[rows, :] = finished(sums, HALF, real)
+        copy = pltpu.make_async_copy(rows_ref.at[rows, :], out_ref.at[rows, :], sems.at[0])
+        copy.start()
+        for b in range(2):
             tile = q_ref[HALF:, :].astype(jnp.float32)
-            came = jnp.sum(jnp.where(iota(tile.shape, 0) < 3, tile, 0.0), axis=0, keepdims=True)
-            density = along_lanes(dens_ref[pl.ds(near, BLOCK), :]) + came[:, 0:BLOCK]
-            put_logs(place_ref, s[PAR], logs_of(density, real))
-            log_copy.start()
-            copy.wait()
-            log_copy.wait()
-
-        @pl.when(jnp.logical_not(sums_came))
-        def _():
-            log_copy.start()
-            log_copy.wait()
+            pieces = jnp.where(iota(tile.shape, 0) < 3, tile, 0.0)
+            more = jnp.sum(pieces, axis=0, keepdims=True)[:, 0:BLOCK]
+            density = along_lanes(dens_ref[b * BLOCK : (b + 1) * BLOCK, :])
+            density = density + jnp.where(s[PAR] == b, more, 0.0)
+            put_logs(log_ref, b, logs_of(density, s[V0 + b]))
+        log_copy.start()
+        copy.wait()
+        log_copy.wait()
 
 
 def call(kernel, us, in_spaces, operands, outs, out_spaces="", aliases=None, scratch=()):
@@ -483,34 +481,48 @@
     qb = over_edge(second)
     sib = to_sibling(x)
     dens, acc = call(own_kernel, 60, "sv", (table, x), state)
-    dens, acc = call(
-        beside_kernel, 13.0, "svvvv", (table, x, sib, dens, acc), state, aliases={3: 0, 4: 1}
+    third, fourth, dens, acc = call(
+        beside_kernel,
+        13.0,
+        "svvvv",
+        (table, x, sib, dens, acc),
+        [bf16(HALF), bf16(HALF + TILE)] + state,
+        aliases={3: 2, 4: 3},
     )
     third, dens_a = call(
         third_kernel,
         10.0,
-        "svvv",
-        (table, qa, after(x, acc), sib),
+        "svvvv",
+        (table, qa, x, sib, third),
         [bf16(HALF), f32(HALF, LANES)],
+        aliases={4: 0},
     )
     qc = over_edge(third)
     dens, acc, _ = lax.optimization_barrier((dens, acc, third))
     dens, acc = call(
         middle_kernel, 15.0, "svvvvv", (table, x, sib, qa, dens, acc), state, aliases={4: 0, 5: 1}
     )
-    fourth, _ = call(
+    (fourth,) = call(
         fourth_kernel,
         10.0,
-        "svvvv",
-        (table, qb, after(x, acc), sib, dens_a),
-        [bf16(HALF + TILE), f32(HALF, LANES)],
+        "svvvvv",
+        (table, qb, after(x, acc), sib, dens_a, fourth),
+        [bf16(HALF + TILE)],
+        aliases={5: 0},
+        scratch=(pltpu.VMEM((HALF, LANES), jnp.float32),),
     )
     dens, acc, fourth = lax.optimization_barrier((dens, acc, fourth))
     qd = over_edge(fourth)
     fa = to_sibling(after(qa, fourth))
     fb = to_sibling(after(qb, fourth))
-    dens, acc = call(
-        outer_kernel, 15.0, "svvvvv", (table, x, qa, qb, dens, acc), state, aliases={4: 0, 5: 1}
+    came, dens, acc = call(
+        outer_kernel,
+        15.0,
+        "svvvvv",
+        (table, x, qa, qb, dens, acc),
+        [jax.ShapeDtypeStruct((2,), jnp.int32)] + state,
+        "svv",
+        aliases={4: 1, 5: 2},
     )
     dens, acc = call(
         forward_kernel,
@@ -520,29 +532,26 @@
         state,
         aliases={5: 0, 6: 1},
     )
+    log_shape = f32(2 * BLOCK // LANES, LANES)
     logs, sums, dens, acc = call(
         far_kernel,
         5.0,
-        "svvvvv",
-        (table, x, qb, qc, dens, acc),
-        [f32(2 * BLOCK // LANES, LANES), bf16(2 * BLOCK)] + state,
-        "vhvv",
+        "ssvvvv",
+        (table, came, x, qc, dens, acc),
+        [log_shape, bf16(2 * BLOCK)] + state,
+        "hhvv",
         aliases={4: 2, 5: 3},
-        scratch=(vmem(2 * BLOCK), dma(2)),
+        scratch=(vmem(2 * BLOCK), pltpu.VMEM(log_shape.shape, jnp.float32), dma(3)),
     )
     logs, sums = call(
         last_kernel,
         5.0,
-        "svvvvvvh",
-        (table, x, qb, qd, dens, acc, logs, sums),
-        [f32(2 * BLOCK // LANES, LANES), bf16(2 * BLOCK)],
+        "ssvvvvhh",
+        (table, came, x, qd, dens, acc, logs, sums),
+        [log_shape, bf16(2 * BLOCK)],
         "hh",
-        aliases={7: 1},
-        scratch=(
-            vmem(2 * BLOCK),
-            pltpu.VMEM((2 * BLOCK // LANES, LANES), jnp.float32),
-            dma(5),
-        ),
+        aliases={6: 0, 7: 1},
+        scratch=(vmem(2 * BLOCK), pltpu.VMEM(log_shape.shape, jnp.float32), dma(5)),
     )
     return logs.reshape(-1), sums
 

time: 45 us -> 44.7 us (level)
  the two profiles are of different devices: /device:TPU:17 before, /device:TPU:14 now
where the time goes in v1:
time: 44.7 us; the launch traced here: 44 us
  Pallas kernels  20 us (45%)
  starting transfers between devices  13.8 us (31%)
  waiting for transfers between devices  8.61 us (19%)
  between operations  1.57 us (4%)
    pallas_call x11, Pallas kernels, call(): pl.pallas_call(kernel, in_specs=[spaces[c] for c in in_spaces], out_specs...  20 us
    ppermute x4, starting transfers between devices, over_edge(): return lax.ppermute(block, 'cluster', edges)  12.5 us
    ppermute x4, waiting for transfers between devices, over_edge(): return lax.ppermute(block, 'cluster', edges)  8.13 us
    ppermute x3, starting transfers between devices, to_sibling(): return lax.ppermute(block, 'cluster', inchip)  1.37 us
  transfers between devices with their start and end apart: 7, of which 4 were waited for; matrix products, arithmetic and copies ran while one was open for 0% of the time, Pallas kernels for 39%

profile of v1, /device:TPU:14, one launch (start us, length us, event | category | flops | bytes accessed | tf_op | source)
XLA Modules:
  0.0 44.0 jit_solution(61652199481128368)
XLA Ops:
  0.6 1.2 %shard_map.59 = bf16[256,768]{1,0:T(8,128)(2,1)S(1)} custom-call(s32[1]{0:T(128)} %bitcast.idx_ref, s32[8,128]{1,0:T(8,128)} %bitcast.4, bf16[1024,768]{1,0:T(8,128)(2,1)} %embed_ref.3), custom_call_target="tpu_custom_call" | custom-call | flops 6899999744 | bytes 1024 | tf_op jit(solution)/shard_map/pallas_call | solution.py:416
  1.8 1.9 %collective-permute-start = (bf16[256,768]{1,0:T(8,128)(2,1)S(1)}, bf16[256,768]{1,0:T(8,128)(2,1)S(1)}, u32[]{:S(2)}, u32[]{:S(2)}) collective-permute-start(bf16[256,768]{1,0:T(8,128)(2,1)S(1)} %shard_map.59), channel_id=1, source_target_pairs={{1,2},{3,4},{5,6},{7,8},{9,10},{11,12},{13,14},{2,1},{4,3},{6,5},{... | collective-permute-start | bytes 1179656 | tf_op jit(solution)/shard_map/ppermute | solution.py:446
  4.4 2.2 %shard_map.60 = (s32[8]{0:T(128)S(1)}, bf16[1040,768]{1,0:T(8,128)(2,1)S(1)}, bf16[256,768]{1,0:T(8,128)(2,1)S(1)}) custom-call(s32[1]{0:T(128)} %bitcast.idx_ref, s32[2,7]{1,0:T(2,128)} %bitcast.6, s32[1]{0:T(128)S(6)} %copy.34.count_ref, s32[8,128]{1,0:T(8,128)} %bitcast.5, bf16[1024,768]{1,0:T(8,128)(2,1)} %embed_ref.3), custom_call_target="tpu_custom_call" | custom-call | flops 16099999744 | bytes 1024 | tf_op jit(solution)/shard_map/pallas_call | solution.py:416
  6.6 3.6 %collective-permute-start.1 = (bf16[256,768]{1,0:T(8,128)(2,1)S(1)}, bf16[256,768]{1,0:T(8,128)(2,1)S(1)}, u32[]{:S(2)}, u32[]{:S(2)}) collective-permute-start(bf16[256,768]{1,0:T(8,128)(2,1)S(1)} %get-tuple-element.38), channel_id=1, source_target_pairs={{1,2},{3,4},{5,6},{7,8},{9,10},{11,12},{13,14},{2,1},{4,3},{6,5},{... | collective-permute-start | bytes 1179656 | tf_op jit(solution)/shard_map/ppermute | solution.py:446
  10.3 0.8 %collective-permute-start.2 = (bf16[1040,768]{1,0:T(8,128)(2,1)S(1)}, bf16[1040,768]{1,0:T(8,128)(2,1)S(1)}, u32[]{:S(2)}, u32[]{:S(2)}) collective-permute-start(bf16[1040,768]{1,0:T(8,128)(2,1)S(1)} %get-tuple-element.49.x_ref), channel_id=1, source_target_pairs={{0,1},{1,0},{2,3},{3,2},{4,5},{5,4},{6,7},{7,6},{8,9},{9,8},{10,11... | collective-permute-start | bytes 4792328 | tf_op jit(solution)/shard_map/ppermute | solution.py:449
  11.1 2.6 %shard_map.61 = (f32[1024,128]{1,0:T(8,128)S(1)}, f32[1024,768]{1,0:T(8,128)S(1)}) custom-call(s32[8]{0:T(128)S(1)} %get-tuple-element.36.s, bf16[1040,768]{1,0:T(8,128)(2,1)S(1)} %get-tuple-element.49.x_ref), custom_call_target="tpu_custom_call" | custom-call | flops 69000003584 | bytes 1024 | tf_op jit(solution)/shard_map/pallas_call | solution.py:416
  13.7 0.5 %collective-permute-done.2.sib_ref = bf16[1040,768]{1,0:T(8,128)(2,1)S(1)} collective-permute-done((bf16[1040,768]{1,0:T(8,128)(2,1)S(1)}, bf16[1040,768]{1,0:T(8,128)(2,1)S(1)}, u32[]{:S(2)}, u32[]{:S(2)}) %collective-permute-start.2) | collective-permute-done | bytes 1597472 | tf_op jit(solution)/shard_map/ppermute | solution.py:449
  14.2 2.3 %shard_map.62 = (bf16[256,768]{1,0:T(8,128)(2,1)S(1)}, bf16[272,768]{1,0:T(8,128)(2,1)S(1)}, f32[1024,128]{1,0:T(8,128)S(1)}, f32[1024,768]{1,0:T(8,128)S(1)}) custom-call(s32[8]{0:T(128)S(1)} %get-tuple-element.36.s, bf16[1040,768]{1,0:T(8,128)(2,1)S(1)} %get-tuple-element.49.x_ref, ...), custom_call_target="tpu_custom_call", output_to_operand_aliasing={{2}: (3, {}), {3}: (4, {})} | custom-call | flops 14949999616 | bytes 1024 | tf_op jit(solution)/shard_map/pallas_call | solution.py:416
  16.4 2.9 %collective-permute-done.q_ref.qa_ref = bf16[256,768]{1,0:T(8,128)(2,1)S(1)} collective-permute-done((bf16[256,768]{1,0:T(8,128)(2,1)S(1)}, bf16[256,768]{1,0:T(8,128)(2,1)S(1)}, u32[]{:S(2)}, u32[]{:S(2)}) %collective-permute-start) | collective-permute-done | bytes 393248 | tf_op jit(solution)/shard_map/ppermute | solution.py:446
  19.4 0.6 %shard_map.63 = (bf16[256,768]{1,0:T(8,128)(2,1)S(1)}, f32[256,128]{1,0:T(8,128)S(1)}) custom-call(s32[8]{0:T(128)S(1)} %get-tuple-element.36.s, bf16[256,768]{1,0:T(8,128)(2,1)S(1)} %collective-permute-done.q_ref.qa_ref, bf16[1040,768]{1,0:T(8,128)(2,1)S(1)} %get-tuple-element.49.x_ref, ...), custom_call_target="tpu_custom_call", output_to_operand_aliasing={{0}: (4, {})} | custom-call | flops 11500000256 | bytes 1024 | tf_op jit(solution)/shard_map/pallas_call | solution.py:416
  19.9 3.5 %collective-permute-start.4 = (bf16[256,768]{1,0:T(8,128)(2,1)S(1)}, bf16[256,768]{1,0:T(8,128)(2,1)S(1)}, u32[]{:S(2)}, u32[]{:S(2)}) collective-permute-start(bf16[256,768]{1,0:T(8,128)(2,1)S(1)} %get-tuple-element.44), channel_id=1, source_target_pairs={{1,2},{3,4},{5,6},{7,8},{9,10},{11,12},{13,14},{2,1},{4,3},{6,5},{... | collective-permute-start | bytes 1179656 | tf_op jit(solution)/shard_map/ppermute | solution.py:446
  23.4 2.2 %shard_map.64 = (f32[1024,128]{1,0:T(8,128)S(1)}, f32[1024,768]{1,0:T(8,128)S(1)}) custom-call(s32[8]{0:T(128)S(1)} %get-tuple-element.36.s, bf16[1040,768]{1,0:T(8,128)(2,1)S(1)} %get-tuple-element.49.x_ref, bf16[1040,768]{1,0:T(8,128)(2,1)S(1)} %collective-permute-done.2.sib_ref, ...), custom_call_target="tpu_custom_call", output_to_operand_aliasing={{0}: (4, {}), {1}: (5, {})} | custom-call | flops 17250000896 | bytes 1024 | tf_op jit(solution)/shard_map/pallas_call | solution.py:416
  25.6 0.0 collective-permute-done.1.q_ref.qb_ref
  25.6 0.6 %shard_map.65 = bf16[272,768]{1,0:T(8,128)(2,1)S(1)} custom-call(s32[8]{0:T(128)S(1)} %get-tuple-element.36.s, bf16[256,768]{1,0:T(8,128)(2,1)S(1)} %collective-permute-done.1.q_ref.qb_ref, bf16[1040,768]{1,0:T(8,128)(2,1)S(1)} %get-tuple-element.49.x_ref, bf16[1040,768]{1,0:T(8,128)(2,1)S(1)} %collective-permute-done.2.sib_ref, ...), custom_call_target="tpu_custom_call", output_to_operand_aliasing={{}: (5, {})} | custom-call | flops 11500000256 | bytes 1024 | tf_op jit(solution)/shard_map/pallas_call | solution.py:416
  26.2 3.4 %collective-permute-start.3 = (bf16[272,768]{1,0:T(8,128)(2,1)S(1)}, bf16[272,768]{1,0:T(8,128)(2,1)S(1)}, u32[]{:S(2)}, u32[]{:S(2)}) collective-permute-start(bf16[272,768]{1,0:T(8,128)(2,1)S(1)} %shard_map.65), channel_id=1, source_target_pairs={{1,2},{3,4},{5,6},{7,8},{9,10},{11,12},{13,14},{2,1},{4,3},{6,5},{... | collective-permute-start | bytes 1253384 | tf_op jit(solution)/shard_map/ppermute | solution.py:446
  29.6 0.4 collective-permute-start.5
  30.1 0.2 collective-permute-start.6
  30.2 2.6 %shard_map.66 = (s32[2]{0:T(128)S(1)}, f32[1024,128]{1,0:T(8,128)S(1)}, f32[1024,768]{1,0:T(8,128)S(1)}) custom-call(s32[8]{0:T(128)S(1)} %get-tuple-element.36.s, bf16[1040,768]{1,0:T(8,128)(2,1)S(1)} %get-tuple-element.49.x_ref, bf16[256,768]{1,0:T(8,128)(2,1)S(1)} %collective-permute-done.q_ref.qa_ref, ...), custom_call_target="tpu_custom_call", output_to_operand_aliasing={{1}: (4, {}), {2}: (5, {})} | custom-call | flops 17250000896 | bytes 1024 | tf_op jit(solution)/shard_map/pallas_call | solution.py:416
  32.8 0.0 collective-permute-done.5.fa_ref
  32.9 2.0 %shard_map.67 = (f32[1024,128]{1,0:T(8,128)S(1)}, f32[1024,768]{1,0:T(8,128)S(1)}) custom-call(s32[8]{0:T(128)S(1)} %get-tuple-element.36.s, bf16[1040,768]{1,0:T(8,128)(2,1)S(1)} %get-tuple-element.49.x_ref, bf16[1040,768]{1,0:T(8,128)(2,1)S(1)} %collective-permute-done.2.sib_ref, ...), custom_call_target="tpu_custom_call", output_to_operand_aliasing={{0}: (5, {}), {1}: (6, {})} | custom-call | flops 17250000896 | bytes 1024 | tf_op jit(solution)/shard_map/pallas_call | solution.py:416
  34.9 2.8 %collective-permute-done.4.q_ref = bf16[256,768]{1,0:T(8,128)(2,1)S(1)} collective-permute-done((bf16[256,768]{1,0:T(8,128)(2,1)S(1)}, bf16[256,768]{1,0:T(8,128)(2,1)S(1)}, u32[]{:S(2)}, u32[]{:S(2)}) %collective-permute-start.4) | collective-permute-done | bytes 393248 | tf_op jit(solution)/shard_map/ppermute | solution.py:446
  37.7 2.1 %shard_map.68 = (f32[8,128]{1,0:T(8,128)}, bf16[1024,768]{1,0:T(8,128)(2,1)}, f32[1024,128]{1,0:T(8,128)S(1)}, f32[1024,768]{1,0:T(8,128)S(1)}) custom-call(s32[8]{0:T(128)S(1)} %get-tuple-element.36.s, s32[2]{0:T(128)S(1)} %get-tuple-element.54.came, bf16[1040,768]{1,0:T(8,128)(2,1)S(1)} %get-tuple-element.49.x_ref, ...), custom_call_target="tpu_custom_call", output_to_operand_aliasing={{2}: (4, {}), {3}: (5, {})} | custom-call | flops 5750000128 | bytes 1024 | tf_op jit(solution)/shard_map/pallas_call | solution.py:416
  39.8 2.3 %collective-permute-done.3.q_ref = bf16[272,768]{1,0:T(8,128)(2,1)S(1)} collective-permute-done((bf16[272,768]{1,0:T(8,128)(2,1)S(1)}, bf16[272,768]{1,0:T(8,128)(2,1)S(1)}, u32[]{:S(2)}, u32[]{:S(2)}) %collective-permute-start.3) | collective-permute-done | bytes 417824 | tf_op jit(solution)/shard_map/ppermute | solution.py:446
  42.2 1.7 %shard_map.69 = (f32[8,128]{1,0:T(8,128)}, bf16[1024,768]{1,0:T(8,128)(2,1)}) custom-call(s32[8]{0:T(128)S(1)} %get-tuple-element.36.s, s32[2]{0:T(128)S(1)} %get-tuple-element.54.came, bf16[1040,768]{1,0:T(8,128)(2,1)S(1)} %get-tuple-element.49.x_ref, ...), custom_call_target="tpu_custom_call", output_to_operand_aliasing={{0}: (6, {}), {1}: (7, {})} | custom-call | flops 5750000128 | bytes 1024 | tf_op jit(solution)/shard_map/pallas_call | solution.py:416
  (1 shorter events, 0.0 us)
Async XLA Ops:
  1.8 17.5 %collective-permute-start = (bf16[256,768]{1,0:T(8,128)(2,1)S(1)}, bf16[256,768]{1,0:T(8,128)(2,1)S(1)}, u32[]{:S(2)}, u32[]{:S(2)}) collective-permute-start(bf16[256,768]{1,0:T(8,128)(2,1)S(1)} %shard_map.59), channel_id=1, source_target_pairs={{1,2},{3,4},{5,6},{7,8},{9,10},{11,12},{13,14},{2,1},{4,3},{6,5},{... | collective-permute-start | bytes 1179656 | tf_op jit(solution)/shard_map/ppermute | solution.py:446
  6.6 19.0 %collective-permute-start.1 = (bf16[256,768]{1,0:T(8,128)(2,1)S(1)}, bf16[256,768]{1,0:T(8,128)(2,1)S(1)}, u32[]{:S(2)}, u32[]{:S(2)}) collective-permute-start(bf16[256,768]{1,0:T(8,128)(2,1)S(1)} %get-tuple-element.38), channel_id=1, source_target_pairs={{1,2},{3,4},{5,6},{7,8},{9,10},{11,12},{13,14},{2,1},{4,3},{6,5},{... | collective-permute-start | bytes 1179656 | tf_op jit(solution)/shard_map/ppermute | solution.py:446
  10.3 3.9 %collective-permute-start.2 = (bf16[1040,768]{1,0:T(8,128)(2,1)S(1)}, bf16[1040,768]{1,0:T(8,128)(2,1)S(1)}, u32[]{:S(2)}, u32[]{:S(2)}) collective-permute-start(bf16[1040,768]{1,0:T(8,128)(2,1)S(1)} %get-tuple-element.49.x_ref), channel_id=1, source_target_pairs={{0,1},{1,0},{2,3},{3,2},{4,5},{5,4},{6,7},{7,6},{8,9},{9,8},{10,11... | collective-permute-start | bytes 4792328 | tf_op jit(solution)/shard_map/ppermute | solution.py:449
  19.9 17.8 %collective-permute-start.4 = (bf16[256,768]{1,0:T(8,128)(2,1)S(1)}, bf16[256,768]{1,0:T(8,128)(2,1)S(1)}, u32[]{:S(2)}, u32[]{:S(2)}) collective-permute-start(bf16[256,768]{1,0:T(8,128)(2,1)S(1)} %get-tuple-element.44), channel_id=1, source_target_pairs={{1,2},{3,4},{5,6},{7,8},{9,10},{11,12},{13,14},{2,1},{4,3},{6,5},{... | collective-permute-start | bytes 1179656 | tf_op jit(solution)/shard_map/ppermute | solution.py:446
  26.2 16.0 %collective-permute-start.3 = (bf16[272,768]{1,0:T(8,128)(2,1)S(1)}, bf16[272,768]{1,0:T(8,128)(2,1)S(1)}, u32[]{:S(2)}, u32[]{:S(2)}) collective-permute-start(bf16[272,768]{1,0:T(8,128)(2,1)S(1)} %shard_map.65), channel_id=1, source_target_pairs={{1,2},{3,4},{5,6},{7,8},{9,10},{11,12},{13,14},{2,1},{4,3},{6,5},{... | collective-permute-start | bytes 1253384 | tf_op jit(solution)/shard_map/ppermute | solution.py:446
  29.6 3.2 %collective-permute-start.5 = (bf16[256,768]{1,0:T(8,128)(2,1)S(1)}, bf16[256,768]{1,0:T(8,128)(2,1)S(1)}, u32[]{:S(2)}, u32[]{:S(2)}) collective-permute-start(bf16[256,768]{1,0:T(8,128)(2,1)S(1)} %collective-permute-done.q_ref.qa_ref), channel_id=1, source_target_pairs={{0,1},{1,0},{2,3},{3,2},{4,5},{5,4},{6,7},{7,6},{8,9},{9,8},{10,11... | collective-permute-start | bytes 1179656 | tf_op jit(solution)/shard_map/ppermute | solution.py:449
  30.1 2.8 %collective-permute-start.6 = (bf16[256,768]{1,0:T(8,128)(2,1)S(1)}, bf16[256,768]{1,0:T(8,128)(2,1)S(1)}, u32[]{:S(2)}, u32[]{:S(2)}) collective-permute-start(bf16[256,768]{1,0:T(8,128)(2,1)S(1)} %collective-permute-done.1.q_ref.qb_ref), channel_id=1, source_target_pairs={{0,1},{1,0},{2,3},{3,2},{4,5},{5,4},{6,7},{7,6},{8,9},{9,8},{10,11... | collective-permute-start | bytes 1179656 | tf_op jit(solution)/shard_map/ppermute | solution.py:449

commit v2 on v1

--- a/solution.py
+++ b/solution.py
@@ -173,36 +173,38 @@
     second_ref[...] = jnp.where(apart, mark, rows).astype(jnp.bfloat16)
 
 
+def own_block(s, b, x_ref, dens_ref, acc_ref):
+    rows = x_ref[b * BLOCK : (b + 1) * BLOCK, :]
+    dens, sums = terms(rows, rows, s[V0 + b])
+    dens_ref[b * BLOCK : (b + 1) * BLOCK, :] = dens
+    acc_ref[b * BLOCK : (b + 1) * BLOCK, :] = sums
+
+
 def own_kernel(s, x_ref, dens_ref, acc_ref):
-    for b in range(2):
-        rows = x_ref[b * BLOCK : (b + 1) * BLOCK, :]
-        dens, sums = terms(rows, rows, s[V0 + b])
-        dens_ref[b * BLOCK : (b + 1) * BLOCK, :] = dens
-        acc_ref[b * BLOCK : (b + 1) * BLOCK, :] = sums
-
-    @pl.when(s[E0] == 1)
-    def _():
-        for b in range(2):
-            other = x_ref[(1 - b) * BLOCK : (2 - b) * BLOCK, :]
-            add_terms(x_ref, (b * BLOCK,), [(other, s[V0 + 1 - b])], dens_ref, acc_ref)
-
-
-def add_sibling(s, start, use, x_ref, sib_ref, dens_ref, acc_ref):
-    @pl.when(use)
-    def _():
-        count = real_rows(sib_ref, start, BLOCK)
-        rights = [(sib_ref[pl.ds(start, BLOCK), :], count)]
-        add_linked(s, at(1 - s[PAR]), at(s[PAR]), x_ref, rights, dens_ref, acc_ref)
-
-
-def beside_kernel(s, x_ref, sib_ref, dens_in, acc_in, third_ref, fourth_ref, dens_ref, acc_ref):
+    own_block(s, 0, x_ref, dens_ref, acc_ref)
+
+
+def cross_kernel(s, x_ref, dens_in, acc_in, third_ref, fourth_ref, dens_ref, acc_ref):
+    own_block(s, 1, x_ref, dens_ref, acc_ref)
     far = at(1 - s[PAR])
     keep = jnp.logical_and(s[E0] == 1, jnp.logical_or(s[PAR] == 0, s[E1] == 1))
     for half, ref in enumerate((third_ref, fourth_ref)):
         rows = x_ref[pl.ds(far + half * HALF, HALF), :].astype(jnp.float32)
         ref[0:HALF, :] = marked(rows, jnp.where(keep, BLOCK, 0))
-    inner, outer = sibling_links(s, sib_ref)
-    add_sibling(s, at(s[PAR]), joined(s, outer), x_ref, sib_ref, dens_ref, acc_ref)
+
+    @pl.when(s[E0] == 1)
+    def _():
+        for b in range(2):
+            other = x_ref[(1 - b) * BLOCK : (2 - b) * BLOCK, :]
+            add_terms(x_ref, (b * BLOCK,), [(other, s[V0 + 1 - b])], dens_ref, acc_ref)
+
+
+def add_sibling(s, start, use, x_ref, sib_ref, dens_ref, acc_ref):
+    @pl.when(use)
+    def _():
+        count = real_rows(sib_ref, start, BLOCK)
+        rights = [(sib_ref[pl.ds(start, BLOCK), :], count)]
+        add_linked(s, at(1 - s[PAR]), at(s[PAR]), x_ref, rights, dens_ref, acc_ref)
 
 
 def not_apart(qb_ref):
@@ -219,8 +221,9 @@
 def middle_kernel(s, x_ref, sib_ref, qa_ref, dens_in, acc_in, dens_ref, acc_ref):
     inner, outer = sibling_links(s, sib_ref)
     near, far = at(s[PAR]), at(1 - s[PAR])
-    use = jnp.logical_and(joined(s, outer), inner)
-    add_sibling(s, far, use, x_ref, sib_ref, dens_ref, acc_ref)
+    meet = joined(s, outer)
+    add_sibling(s, near, meet, x_ref, sib_ref, dens_ref, acc_ref)
+    add_sibling(s, far, jnp.logical_and(meet, inner), x_ref, sib_ref, dens_ref, acc_ref)
 
     @pl.when(jnp.logical_and(s[PAR] == 1, s[E1] == 1))
     def _():
@@ -322,7 +325,7 @@
 
 
 def far_kernel(
-    s, came, x_ref, q_ref, dens_in, acc_in, log_out, out_ref, dens_ref, acc_ref,
+    s, came, x_ref, q_ref, dens_in, acc_in, lanes_ref, log_out, out_ref, dens_ref, acc_ref,
     rows_ref, log_ref, sems
 ):
     near, far = at(s[PAR]), at(1 - s[PAR])
@@ -347,6 +350,7 @@
             copies.append(copy)
         for b in range(2):
             density = along_lanes(dens_ref[b * BLOCK : (b + 1) * BLOCK, :])
+            lanes_ref[b : b + 1, :] = density
             put_logs(log_ref, b, logs_of(density, s[V0 + b]))
         copy = pltpu.make_async_copy(log_ref, log_out, sems.at[2])
         copy.start()
@@ -355,7 +359,7 @@
 
 
 def last_kernel(
-    s, came, x_ref, q_ref, dens_ref, acc_ref, log_in, out_in, log_out, out_ref,
+    s, came, x_ref, q_ref, lanes_ref, dens_ref, acc_ref, log_in, out_in, log_out, out_ref,
     rows_ref, log_ref, sems
 ):
     log_copy = pltpu.make_async_copy(log_ref, log_out, sems.at[4])
@@ -398,12 +402,11 @@
         rows_ref[rows, :] = finished(sums, HALF, real)
         copy = pltpu.make_async_copy(rows_ref.at[rows, :], out_ref.at[rows, :], sems.at[0])
         copy.start()
-        for b in range(2):
-            tile = q_ref[HALF:, :].astype(jnp.float32)
-            pieces = jnp.where(iota(tile.shape, 0) < 3, tile, 0.0)
-            more = jnp.sum(pieces, axis=0, keepdims=True)[:, 0:BLOCK]
-            density = along_lanes(dens_ref[b * BLOCK : (b + 1) * BLOCK, :])
-            density = density + jnp.where(s[PAR] == b, more, 0.0)
+        tile = q_ref[HALF:, :].astype(jnp.float32)
+        pieces = jnp.where(iota(tile.shape, 0) < 3, tile, 0.0)
+        more = jnp.sum(pieces, axis=0, keepdims=True)[:, 0:BLOCK]
+        for b in range(2):
+            density = lanes_ref[b : b + 1, :] + jnp.where(s[PAR] == b, more, 0.0)
             put_logs(log_ref, b, logs_of(density, s[V0 + b]))
         log_copy.start()
         copy.wait()
@@ -478,16 +481,17 @@
             dma(6),
         ),
     )
+    sib = to_sibling(x)
+    dens, acc = call(own_kernel, 30.0, "sv", (table, x), state)
+    dens, acc, second = lax.optimization_barrier((dens, acc, second))
     qb = over_edge(second)
-    sib = to_sibling(x)
-    dens, acc = call(own_kernel, 60, "sv", (table, x), state)
     third, fourth, dens, acc = call(
-        beside_kernel,
+        cross_kernel,
         13.0,
-        "svvvv",
-        (table, x, sib, dens, acc),
+        "svvv",
+        (table, x, dens, acc),
         [bf16(HALF), bf16(HALF + TILE)] + state,
-        aliases={3: 2, 4: 3},
+        aliases={2: 2, 3: 3},
     )
     third, dens_a = call(
         third_kernel,
@@ -533,24 +537,24 @@
         aliases={5: 0, 6: 1},
     )
     log_shape = f32(2 * BLOCK // LANES, LANES)
-    logs, sums, dens, acc = call(
+    lanes, logs, sums, dens, acc = call(
         far_kernel,
         5.0,
         "ssvvvv",
         (table, came, x, qc, dens, acc),
-        [log_shape, bf16(2 * BLOCK)] + state,
-        "hhvv",
-        aliases={4: 2, 5: 3},
+        [f32(8, BLOCK), log_shape, bf16(2 * BLOCK)] + state,
+        "vhhvv",
+        aliases={4: 3, 5: 4},
         scratch=(vmem(2 * BLOCK), pltpu.VMEM(log_shape.shape, jnp.float32), dma(3)),
     )
     logs, sums = call(
         last_kernel,
         5.0,
-        "ssvvvvhh",
-        (table, came, x, qd, dens, acc, logs, sums),
+        "ssvvvvvhh",
+        (table, came, x, qd, lanes, dens, acc, logs, sums),
         [log_shape, bf16(2 * BLOCK)],
         "hh",
-        aliases={6: 0, 7: 1},
+        aliases={7: 0, 8: 1},
         scratch=(vmem(2 * BLOCK), pltpu.VMEM(log_shape.shape, jnp.float32), dma(5)),
     )
     return logs.reshape(-1), sums

time: 44.7 us -> 43.4 us (0.971)
  the two profiles are of different devices: /device:TPU:14 before, /device:TPU:19 now
where the time goes in v2:
time: 43.4 us; the launch traced here: 42.6 us
  starting transfers between devices  18.3 us (42%)
  Pallas kernels  18.1 us (42%)
  waiting for transfers between devices  4.7 us (11%)
  between operations  1.6 us (4%)
    pallas_call x11, Pallas kernels, call(): pl.pallas_call(kernel, in_specs=[spaces[c] for c in in_spaces], out_specs...  18.1 us
    ppermute x4, starting transfers between devices, over_edge(): return lax.ppermute(block, 'cluster', edges)  17.6 us
    ppermute x4, waiting for transfers between devices, over_edge(): return lax.ppermute(block, 'cluster', edges)  4.69 us
  transfers between devices with their start and end apart: 7, of which 2 were waited for; matrix products, arithmetic and copies ran while one was open for 0% of the time, Pallas kernels for 36%

profile of v2, /device:TPU:19, one launch (start us, length us, event | category | flops | bytes accessed | tf_op | source)
XLA Modules:
  0.0 42.6 jit_solution(6366716544143393251)
XLA Ops:
  0.6 1.2 %shard_map.59 = bf16[256,768]{1,0:T(8,128)(2,1)S(1)} custom-call(s32[1]{0:T(128)} %bitcast.idx_ref, s32[8,128]{1,0:T(8,128)} %bitcast.4, bf16[1024,768]{1,0:T(8,128)(2,1)} %embed_ref.3), custom_call_target="tpu_custom_call" | custom-call | flops 6899999744 | bytes 1024 | tf_op jit(solution)/shard_map/pallas_call | solution.py:419
  1.8 3.7 %collective-permute-start = (bf16[256,768]{1,0:T(8,128)(2,1)S(1)}, bf16[256,768]{1,0:T(8,128)(2,1)S(1)}, u32[]{:S(2)}, u32[]{:S(2)}) collective-permute-start(bf16[256,768]{1,0:T(8,128)(2,1)S(1)} %shard_map.59), channel_id=1, source_target_pairs={{1,2},{3,4},{5,6},{7,8},{9,10},{11,12},{13,14},{2,1},{4,3},{6,5},{... | collective-permute-start | bytes 1179656 | tf_op jit(solution)/shard_map/ppermute | solution.py:449
  6.2 2.2 %shard_map.60 = (s32[8]{0:T(128)S(1)}, bf16[1040,768]{1,0:T(8,128)(2,1)S(1)}, bf16[256,768]{1,0:T(8,128)(2,1)S(1)}) custom-call(s32[1]{0:T(128)} %bitcast.idx_ref, s32[2,7]{1,0:T(2,128)} %bitcast.6, s32[1]{0:T(128)S(6)} %copy.34.count_ref, s32[8,128]{1,0:T(8,128)} %bitcast.5, bf16[1024,768]{1,0:T(8,128)(2,1)} %embed_ref.3), custom_call_target="tpu_custom_call" | custom-call | flops 16099999744 | bytes 1024 | tf_op jit(solution)/shard_map/pallas_call | solution.py:419
  8.4 0.1 collective-permute-start.2
  8.5 1.7 %shard_map.61 = (f32[1024,128]{1,0:T(8,128)S(1)}, f32[1024,768]{1,0:T(8,128)S(1)}) custom-call(s32[8]{0:T(128)S(1)} %get-tuple-element.40.s, bf16[1040,768]{1,0:T(8,128)(2,1)S(1)} %get-tuple-element.56.x_ref), custom_call_target="tpu_custom_call" | custom-call | flops 34500001792 | bytes 1024 | tf_op jit(solution)/shard_map/pallas_call | solution.py:419
  10.2 3.5 %collective-permute-start.1 = (bf16[256,768]{1,0:T(8,128)(2,1)S(1)}, bf16[256,768]{1,0:T(8,128)(2,1)S(1)}, u32[]{:S(2)}, u32[]{:S(2)}) collective-permute-start(bf16[256,768]{1,0:T(8,128)(2,1)S(1)} %get-tuple-element.45), channel_id=1, source_target_pairs={{1,2},{3,4},{5,6},{7,8},{9,10},{11,12},{13,14},{2,1},{4,3},{6,5},{... | collective-permute-start | bytes 1179656 | tf_op jit(solution)/shard_map/ppermute | solution.py:449
  13.7 1.9 %shard_map.62 = (bf16[256,768]{1,0:T(8,128)(2,1)S(1)}, bf16[272,768]{1,0:T(8,128)(2,1)S(1)}, f32[1024,128]{1,0:T(8,128)S(1)}, f32[1024,768]{1,0:T(8,128)S(1)}) custom-call(s32[8]{0:T(128)S(1)} %get-tuple-element.40.s, bf16[1040,768]{1,0:T(8,128)(2,1)S(1)} %get-tuple-element.56.x_ref, ...), custom_call_target="tpu_custom_call", output_to_operand_aliasing={{2}: (2, {}), {3}: (3, {})} | custom-call | flops 14949999616 | bytes 1024 | tf_op jit(solution)/shard_map/pallas_call | solution.py:419
  15.6 0.0 collective-permute-done.q_ref.qa_ref
  15.6 0.0 collective-permute-done.2.sib_ref
  15.6 0.6 %shard_map.63 = (bf16[256,768]{1,0:T(8,128)(2,1)S(1)}, f32[256,128]{1,0:T(8,128)S(1)}) custom-call(s32[8]{0:T(128)S(1)} %get-tuple-element.40.s, bf16[256,768]{1,0:T(8,128)(2,1)S(1)} %collective-permute-done.q_ref.qa_ref, bf16[1040,768]{1,0:T(8,128)(2,1)S(1)} %get-tuple-element.56.x_ref, ...), custom_call_target="tpu_custom_call", output_to_operand_aliasing={{0}: (4, {})} | custom-call | flops 11500000256 | bytes 1024 | tf_op jit(solution)/shard_map/pallas_call | solution.py:419
  16.2 5.4 %collective-permute-start.4 = (bf16[256,768]{1,0:T(8,128)(2,1)S(1)}, bf16[256,768]{1,0:T(8,128)(2,1)S(1)}, u32[]{:S(2)}, u32[]{:S(2)}) collective-permute-start(bf16[256,768]{1,0:T(8,128)(2,1)S(1)} %get-tuple-element.51), channel_id=1, source_target_pairs={{1,2},{3,4},{5,6},{7,8},{9,10},{11,12},{13,14},{2,1},{4,3},{6,5},{... | collective-permute-start | bytes 1179656 | tf_op jit(solution)/shard_map/ppermute | solution.py:449
  21.6 3.4 %shard_map.64 = (f32[1024,128]{1,0:T(8,128)S(1)}, f32[1024,768]{1,0:T(8,128)S(1)}) custom-call(s32[8]{0:T(128)S(1)} %get-tuple-element.40.s, bf16[1040,768]{1,0:T(8,128)(2,1)S(1)} %get-tuple-element.56.x_ref, bf16[1040,768]{1,0:T(8,128)(2,1)S(1)} %collective-permute-done.2.sib_ref, ...), custom_call_target="tpu_custom_call", output_to_operand_aliasing={{0}: (4, {}), {1}: (5, {})} | custom-call | flops 17250000896 | bytes 1024 | tf_op jit(solution)/shard_map/pallas_call | solution.py:419
  25.0 2.8 %collective-permute-done.1.q_ref.qb_ref = bf16[256,768]{1,0:T(8,128)(2,1)S(1)} collective-permute-done((bf16[256,768]{1,0:T(8,128)(2,1)S(1)}, bf16[256,768]{1,0:T(8,128)(2,1)S(1)}, u32[]{:S(2)}, u32[]{:S(2)}) %collective-permute-start.1) | collective-permute-done | bytes 393248 | tf_op jit(solution)/shard_map/ppermute | solution.py:449
  27.9 0.6 %shard_map.65 = bf16[272,768]{1,0:T(8,128)(2,1)S(1)} custom-call(s32[8]{0:T(128)S(1)} %get-tuple-element.40.s, bf16[256,768]{1,0:T(8,128)(2,1)S(1)} %collective-permute-done.1.q_ref.qb_ref, bf16[1040,768]{1,0:T(8,128)(2,1)S(1)} %get-tuple-element.56.x_ref, bf16[1040,768]{1,0:T(8,128)(2,1)S(1)} %collective-permute-done.2.sib_ref, ...), custom_call_target="tpu_custom_call", output_to_operand_aliasing={{}: (5, {})} | custom-call | flops 11500000256 | bytes 1024 | tf_op jit(solution)/shard_map/pallas_call | solution.py:419
  28.4 5.0 %collective-permute-start.3 = (bf16[272,768]{1,0:T(8,128)(2,1)S(1)}, bf16[272,768]{1,0:T(8,128)(2,1)S(1)}, u32[]{:S(2)}, u32[]{:S(2)}) collective-permute-start(bf16[272,768]{1,0:T(8,128)(2,1)S(1)} %shard_map.65), channel_id=1, source_target_pairs={{1,2},{3,4},{5,6},{7,8},{9,10},{11,12},{13,14},{2,1},{4,3},{6,5},{... | collective-permute-start | bytes 1253384 | tf_op jit(solution)/shard_map/ppermute | solution.py:449
  33.4 0.1 collective-permute-start.5
  33.5 0.5 %collective-permute-start.6 = (bf16[256,768]{1,0:T(8,128)(2,1)S(1)}, bf16[256,768]{1,0:T(8,128)(2,1)S(1)}, u32[]{:S(2)}, u32[]{:S(2)}) collective-permute-start(bf16[256,768]{1,0:T(8,128)(2,1)S(1)} %collective-permute-done.1.q_ref.qb_ref), channel_id=1, source_target_pairs={{0,1},{1,0},{2,3},{3,2},{4,5},{5,4},{6,7},{7,6},{8,9},{9,8},{10,11... | collective-permute-start | bytes 1179656 | tf_op jit(solution)/shard_map/ppermute | solution.py:452
  34.0 2.3 %shard_map.66 = (s32[2]{0:T(128)S(1)}, f32[1024,128]{1,0:T(8,128)S(1)}, f32[1024,768]{1,0:T(8,128)S(1)}) custom-call(s32[8]{0:T(128)S(1)} %get-tuple-element.40.s, bf16[1040,768]{1,0:T(8,128)(2,1)S(1)} %get-tuple-element.56.x_ref, bf16[256,768]{1,0:T(8,128)(2,1)S(1)} %collective-permute-done.q_ref.qa_ref, ...), custom_call_target="tpu_custom_call", output_to_operand_aliasing={{1}: (4, {}), {2}: (5, {})} | custom-call | flops 17250000896 | bytes 1024 | tf_op jit(solution)/shard_map/pallas_call | solution.py:419
  36.3 0.0 collective-permute-done.5.fa_ref
  36.3 0.7 %shard_map.67 = (f32[1024,128]{1,0:T(8,128)S(1)}, f32[1024,768]{1,0:T(8,128)S(1)}) custom-call(s32[8]{0:T(128)S(1)} %get-tuple-element.40.s, bf16[1040,768]{1,0:T(8,128)(2,1)S(1)} %get-tuple-element.56.x_ref, bf16[1040,768]{1,0:T(8,128)(2,1)S(1)} %collective-permute-done.2.sib_ref, ...), custom_call_target="tpu_custom_call", output_to_operand_aliasing={{0}: (5, {}), {1}: (6, {})} | custom-call | flops 17250000896 | bytes 1024 | tf_op jit(solution)/shard_map/pallas_call | solution.py:419
  37.0 0.0 collective-permute-done.4.q_ref
  37.0 2.1 %shard_map.68 = (f32[8,512]{1,0:T(8,128)S(1)}, f32[8,128]{1,0:T(8,128)}, bf16[1024,768]{1,0:T(8,128)(2,1)}, f32[1024,128]{1,0:T(8,128)S(1)}, f32[1024,768]{1,0:T(8,128)S(1)}) custom-call(s32[8]{0:T(128)S(1)} %get-tuple-element.40.s, s32[2]{0:T(128)S(1)} %get-tuple-element.61.came, ...), custom_call_target="tpu_custom_call", output_to_operand_aliasing={{3}: (4, {}), {4}: (5, {})} | custom-call | flops 5750000128 | bytes 1024 | tf_op jit(solution)/shard_map/pallas_call | solution.py:419
  39.2 1.9 %collective-permute-done.3.q_ref = bf16[272,768]{1,0:T(8,128)(2,1)S(1)} collective-permute-done((bf16[272,768]{1,0:T(8,128)(2,1)S(1)}, bf16[272,768]{1,0:T(8,128)(2,1)S(1)}, u32[]{:S(2)}, u32[]{:S(2)}) %collective-permute-start.3) | collective-permute-done | bytes 417824 | tf_op jit(solution)/shard_map/ppermute | solution.py:449
  41.0 1.5 %shard_map.69 = (f32[8,128]{1,0:T(8,128)}, bf16[1024,768]{1,0:T(8,128)(2,1)}) custom-call(s32[8]{0:T(128)S(1)} %get-tuple-element.40.s, s32[2]{0:T(128)S(1)} %get-tuple-element.61.came, bf16[1040,768]{1,0:T(8,128)(2,1)S(1)} %get-tuple-element.56.x_ref, ...), custom_call_target="tpu_custom_call", output_to_operand_aliasing={{0}: (7, {}), {1}: (8, {})} | custom-call | flops 5750000128 | bytes 1024 | tf_op jit(solution)/shard_map/pallas_call | solution.py:419
  (1 shorter events, 0.0 us)
Async XLA Ops:
  1.8 13.8 %collective-permute-start = (bf16[256,768]{1,0:T(8,128)(2,1)S(1)}, bf16[256,768]{1,0:T(8,128)(2,1)S(1)}, u32[]{:S(2)}, u32[]{:S(2)}) collective-permute-start(bf16[256,768]{1,0:T(8,128)(2,1)S(1)} %shard_map.59), channel_id=1, source_target_pairs={{1,2},{3,4},{5,6},{7,8},{9,10},{11,12},{13,14},{2,1},{4,3},{6,5},{... | collective-permute-start | bytes 1179656 | tf_op jit(solution)/shard_map/ppermute | solution.py:449
  8.4 7.2 %collective-permute-start.2 = (bf16[1040,768]{1,0:T(8,128)(2,1)S(1)}, bf16[1040,768]{1,0:T(8,128)(2,1)S(1)}, u32[]{:S(2)}, u32[]{:S(2)}) collective-permute-start(bf16[1040,768]{1,0:T(8,128)(2,1)S(1)} %get-tuple-element.56.x_ref), channel_id=1, source_target_pairs={{0,1},{1,0},{2,3},{3,2},{4,5},{5,4},{6,7},{7,6},{8,9},{9,8},{10,11... | collective-permute-start | bytes 4792328 | tf_op jit(solution)/shard_map/ppermute | solution.py:452
  10.2 17.6 %collective-permute-start.1 = (bf16[256,768]{1,0:T(8,128)(2,1)S(1)}, bf16[256,768]{1,0:T(8,128)(2,1)S(1)}, u32[]{:S(2)}, u32[]{:S(2)}) collective-permute-start(bf16[256,768]{1,0:T(8,128)(2,1)S(1)} %get-tuple-element.45), channel_id=1, source_target_pairs={{1,2},{3,4},{5,6},{7,8},{9,10},{11,12},{13,14},{2,1},{4,3},{6,5},{... | collective-permute-start | bytes 1179656 | tf_op jit(solution)/shard_map/ppermute | solution.py:449
  16.2 20.8 %collective-permute-start.4 = (bf16[256,768]{1,0:T(8,128)(2,1)S(1)}, bf16[256,768]{1,0:T(8,128)(2,1)S(1)}, u32[]{:S(2)}, u32[]{:S(2)}) collective-permute-start(bf16[256,768]{1,0:T(8,128)(2,1)S(1)} %get-tuple-element.51), channel_id=1, source_target_pairs={{1,2},{3,4},{5,6},{7,8},{9,10},{11,12},{13,14},{2,1},{4,3},{6,5},{... | collective-permute-start | bytes 1179656 | tf_op jit(solution)/shard_map/ppermute | solution.py:449
  28.4 12.6 %collective-permute-start.3 = (bf16[272,768]{1,0:T(8,128)(2,1)S(1)}, bf16[272,768]{1,0:T(8,128)(2,1)S(1)}, u32[]{:S(2)}, u32[]{:S(2)}) collective-permute-start(bf16[272,768]{1,0:T(8,128)(2,1)S(1)} %shard_map.65), channel_id=1, source_target_pairs={{1,2},{3,4},{5,6},{7,8},{9,10},{11,12},{13,14},{2,1},{4,3},{6,5},{... | collective-permute-start | bytes 1253384 | tf_op jit(solution)/shard_map/ppermute | solution.py:449
  33.4 2.9 %collective-permute-start.5 = (bf16[256,768]{1,0:T(8,128)(2,1)S(1)}, bf16[256,768]{1,0:T(8,128)(2,1)S(1)}, u32[]{:S(2)}, u32[]{:S(2)}) collective-permute-start(bf16[256,768]{1,0:T(8,128)(2,1)S(1)} %collective-permute-done.q_ref.qa_ref), channel_id=1, source_target_pairs={{0,1},{1,0},{2,3},{3,2},{4,5},{5,4},{6,7},{7,6},{8,9},{9,8},{10,11... | collective-permute-start | bytes 1179656 | tf_op jit(solution)/shard_map/ppermute | solution.py:452
  33.5 2.8 %collective-permute-start.6 = (bf16[256,768]{1,0:T(8,128)(2,1)S(1)}, bf16[256,768]{1,0:T(8,128)(2,1)S(1)}, u32[]{:S(2)}, u32[]{:S(2)}) collective-permute-start(bf16[256,768]{1,0:T(8,128)(2,1)S(1)} %collective-permute-done.1.q_ref.qb_ref), channel_id=1, source_target_pairs={{0,1},{1,0},{2,3},{3,2},{4,5},{5,4},{6,7},{7,6},{8,9},{9,8},{10,11... | collective-permute-start | bytes 1179656 | tf_op jit(solution)/shard_map/ppermute | solution.py:452

commit v3 on v2

--- a/solution.py
+++ b/solution.py
@@ -15,7 +15,7 @@
 SHARPNESS = 8.0
 LOG2E = 1.4426950408889634
 
-IDX, PAR, V0, V1, E0, E1, C0, C1 = range(8)
+IDX, PAR, V0, V1, E0, E1, C0, C1, SUMS, ROWS = range(10)
 
 VM = pl.BlockSpec(memory_space=pltpu.VMEM)
 SM = pl.BlockSpec(memory_space=pltpu.SMEM)
@@ -284,8 +284,10 @@
     upper, lone = s[PAR] == 1, s[E0] == 0
     sums = jnp.where(upper, s[C1] == 4, jnp.logical_and(linked, lone))
     rows = jnp.where(upper, s[C1] == 3, jnp.logical_and(linked, jnp.logical_not(lone)))
-    came[0] = sums.astype(jnp.int32)
-    came[1] = rows.astype(jnp.int32)
+    for place in range(8):
+        came[place] = s[place]
+    came[SUMS] = sums.astype(jnp.int32)
+    came[ROWS] = rows.astype(jnp.int32)
     rights = [(ref[...], real_rows(ref, 0, HALF)) for ref in (qa_ref, qb_ref)]
 
     @pl.when(jnp.logical_and(linked, s[PAR] == 0))
@@ -325,19 +327,19 @@
 
 
 def far_kernel(
-    s, came, x_ref, q_ref, dens_in, acc_in, lanes_ref, log_out, out_ref, dens_ref, acc_ref,
+    s, x_ref, q_ref, dens_in, acc_in, lanes_ref, log_out, out_ref, dens_ref, acc_ref,
     rows_ref, log_ref, sems
 ):
     near, far = at(s[PAR]), at(1 - s[PAR])
 
-    @pl.when(came[1] == 1)
+    @pl.when(s[ROWS] == 1)
     def _():
         count = real_rows(q_ref, 0, HALF)
         add_linked(s, near, far, x_ref, [(q_ref[...], count)], dens_ref, acc_ref)
 
-    @pl.when(came[1] == 0)
-    def _():
-        @pl.when(came[0] == 1)
+    @pl.when(s[ROWS] == 0)
+    def _():
+        @pl.when(s[SUMS] == 1)
         def _():
             acc_ref[pl.ds(near, HALF), :] += q_ref[...].astype(jnp.float32)
 
@@ -359,12 +361,12 @@
 
 
 def last_kernel(
-    s, came, x_ref, q_ref, lanes_ref, dens_ref, acc_ref, log_in, out_in, log_out, out_ref,
+    s, x_ref, q_ref, lanes_ref, dens_ref, acc_ref, log_in, out_in, log_out, out_ref,
     rows_ref, log_ref, sems
 ):
     log_copy = pltpu.make_async_copy(log_ref, log_out, sems.at[4])
 
-    @pl.when(came[1] == 1)
+    @pl.when(s[ROWS] == 1)
     def _():
         count = real_rows(q_ref, 0, HALF)
         right = q_ref[0:HALF, :]
@@ -393,7 +395,7 @@
         for copy in copies:
             copy.wait()
 
-    @pl.when(came[0] == 1)
+    @pl.when(s[SUMS] == 1)
     def _():
         near = at(s[PAR])
         real = jnp.where(s[PAR] == 1, s[V1], s[V0])
@@ -524,7 +526,7 @@
         15.0,
         "svvvvv",
         (table, x, qa, qb, dens, acc),
-        [jax.ShapeDtypeStruct((2,), jnp.int32)] + state,
+        [pltpu.SMEM((10,), jnp.int32)] + state,
         "svv",
         aliases={4: 1, 5: 2},
     )
@@ -540,21 +542,21 @@
     lanes, logs, sums, dens, acc = call(
         far_kernel,
         5.0,
-        "ssvvvv",
-        (table, came, x, qc, dens, acc),
+        "svvvv",
+        (came, x, qc, dens, acc),
         [f32(8, BLOCK), log_shape, bf16(2 * BLOCK)] + state,
         "vhhvv",
-        aliases={4: 3, 5: 4},
+        aliases={3: 3, 4: 4},
         scratch=(vmem(2 * BLOCK), pltpu.VMEM(log_shape.shape, jnp.float32), dma(3)),
     )
     logs, sums = call(
         last_kernel,
         5.0,
-        "ssvvvvvhh",
-        (table, came, x, qd, lanes, dens, acc, logs, sums),
+        "svvvvvhh",
+        (came, x, qd, lanes, dens, acc, logs, sums),
         [log_shape, bf16(2 * BLOCK)],
         "hh",
-        aliases={7: 0, 8: 1},
+        aliases={6: 0, 7: 1},
         scratch=(vmem(2 * BLOCK), pltpu.VMEM(log_shape.shape, jnp.float32), dma(5)),
     )
     return logs.reshape(-1), sums

time: 43.4 us -> 42.9 us (0.988)
  the two profiles are of different devices: /device:TPU:19 before, /device:TPU:25 now
where the time goes in v3:
time: 42.9 us; the launch traced here: 43.3 us
  Pallas kernels  17.1 us (40%)
  starting transfers between devices  12.7 us (30%)
  waiting for transfers between devices  11.9 us (28%)
  between operations  1.57 us (4%)
    pallas_call x11, Pallas kernels, call(): pl.pallas_call(kernel, in_specs=[spaces[c] for c in in_spaces], out_specs...  17.1 us
    ppermute x4, starting transfers between devices, over_edge(): return lax.ppermute(block, 'cluster', edges)  12.1 us
    ppermute x4, waiting for transfers between devices, over_edge(): return lax.ppermute(block, 'cluster', edges)  11.8 us
  transfers between devices with their start and end apart: 7, of which 4 were waited for; matrix products, arithmetic and copies ran while one was open for 0% of the time, Pallas kernels for 32%

profile of v3, /device:TPU:25, one launch (start us, length us, event | category | flops | bytes accessed | tf_op | source)
XLA Modules:
  0.0 43.3 jit_solution(14181281990411966738)
XLA Ops:
  0.6 1.2 %shard_map.59 = bf16[256,768]{1,0:T(8,128)(2,1)S(1)} custom-call(s32[1]{0:T(128)} %bitcast.idx_ref, s32[8,128]{1,0:T(8,128)} %bitcast.4, bf16[1024,768]{1,0:T(8,128)(2,1)} %embed_ref.3), custom_call_target="tpu_custom_call" | custom-call | flops 6899999744 | bytes 1024 | tf_op jit(solution)/shard_map/pallas_call | solution.py:421
  1.8 3.7 %collective-permute-start = (bf16[256,768]{1,0:T(8,128)(2,1)S(1)}, bf16[256,768]{1,0:T(8,128)(2,1)S(1)}, u32[]{:S(2)}, u32[]{:S(2)}) collective-permute-start(bf16[256,768]{1,0:T(8,128)(2,1)S(1)} %shard_map.59), channel_id=1, source_target_pairs={{1,2},{3,4},{5,6},{7,8},{9,10},{11,12},{13,14},{2,1},{4,3},{6,5},{... | collective-permute-start | bytes 1179656 | tf_op jit(solution)/shard_map/ppermute | solution.py:451
  6.2 2.2 %shard_map.60 = (s32[8]{0:T(128)S(1)}, bf16[1040,768]{1,0:T(8,128)(2,1)S(1)}, bf16[256,768]{1,0:T(8,128)(2,1)S(1)}) custom-call(s32[1]{0:T(128)} %bitcast.idx_ref, s32[2,7]{1,0:T(2,128)} %bitcast.6, s32[1]{0:T(128)S(6)} %copy.34.count_ref, s32[8,128]{1,0:T(8,128)} %bitcast.5, bf16[1024,768]{1,0:T(8,128)(2,1)} %embed_ref.3), custom_call_target="tpu_custom_call" | custom-call | flops 16099999744 | bytes 1024 | tf_op jit(solution)/shard_map/pallas_call | solution.py:421
  8.4 0.1 collective-permute-start.2
  8.5 1.7 %shard_map.61 = (f32[1024,128]{1,0:T(8,128)S(1)}, f32[1024,768]{1,0:T(8,128)S(1)}) custom-call(s32[8]{0:T(128)S(1)} %get-tuple-element.40.s, bf16[1040,768]{1,0:T(8,128)(2,1)S(1)} %get-tuple-element.56.x_ref), custom_call_target="tpu_custom_call" | custom-call | flops 34500001792 | bytes 1024 | tf_op jit(solution)/shard_map/pallas_call | solution.py:421
  10.2 1.9 %collective-permute-start.1 = (bf16[256,768]{1,0:T(8,128)(2,1)S(1)}, bf16[256,768]{1,0:T(8,128)(2,1)S(1)}, u32[]{:S(2)}, u32[]{:S(2)}) collective-permute-start(bf16[256,768]{1,0:T(8,128)(2,1)S(1)} %get-tuple-element.45), channel_id=1, source_target_pairs={{1,2},{3,4},{5,6},{7,8},{9,10},{11,12},{13,14},{2,1},{4,3},{6,5},{... | collective-permute-start | bytes 1179656 | tf_op jit(solution)/shard_map/ppermute | solution.py:451
  12.1 1.9 %shard_map.62 = (bf16[256,768]{1,0:T(8,128)(2,1)S(1)}, bf16[272,768]{1,0:T(8,128)(2,1)S(1)}, f32[1024,128]{1,0:T(8,128)S(1)}, f32[1024,768]{1,0:T(8,128)S(1)}) custom-call(s32[8]{0:T(128)S(1)} %get-tuple-element.40.s, bf16[1040,768]{1,0:T(8,128)(2,1)S(1)} %get-tuple-element.56.x_ref, ...), custom_call_target="tpu_custom_call", output_to_operand_aliasing={{2}: (2, {}), {3}: (3, {})} | custom-call | flops 14949999616 | bytes 1024 | tf_op jit(solution)/shard_map/pallas_call | solution.py:421
  14.0 1.2 %collective-permute-done.q_ref.qa_ref = bf16[256,768]{1,0:T(8,128)(2,1)S(1)} collective-permute-done((bf16[256,768]{1,0:T(8,128)(2,1)S(1)}, bf16[256,768]{1,0:T(8,128)(2,1)S(1)}, u32[]{:S(2)}, u32[]{:S(2)}) %collective-permute-start) | collective-permute-done | bytes 393248 | tf_op jit(solution)/shard_map/ppermute | solution.py:451
  15.2 0.0 collective-permute-done.2.sib_ref
  15.2 0.6 %shard_map.63 = (bf16[256,768]{1,0:T(8,128)(2,1)S(1)}, f32[256,128]{1,0:T(8,128)S(1)}) custom-call(s32[8]{0:T(128)S(1)} %get-tuple-element.40.s, bf16[256,768]{1,0:T(8,128)(2,1)S(1)} %collective-permute-done.q_ref.qa_ref, bf16[1040,768]{1,0:T(8,128)(2,1)S(1)} %get-tuple-element.56.x_ref, ...), custom_call_target="tpu_custom_call", output_to_operand_aliasing={{0}: (4, {})} | custom-call | flops 11500000256 | bytes 1024 | tf_op jit(solution)/shard_map/pallas_call | solution.py:421
  15.8 4.5 %collective-permute-start.4 = (bf16[256,768]{1,0:T(8,128)(2,1)S(1)}, bf16[256,768]{1,0:T(8,128)(2,1)S(1)}, u32[]{:S(2)}, u32[]{:S(2)}) collective-permute-start(bf16[256,768]{1,0:T(8,128)(2,1)S(1)} %get-tuple-element.51), channel_id=1, source_target_pairs={{1,2},{3,4},{5,6},{7,8},{9,10},{11,12},{13,14},{2,1},{4,3},{6,5},{... | collective-permute-start | bytes 1179656 | tf_op jit(solution)/shard_map/ppermute | solution.py:451
  20.3 3.4 %shard_map.64 = (f32[1024,128]{1,0:T(8,128)S(1)}, f32[1024,768]{1,0:T(8,128)S(1)}) custom-call(s32[8]{0:T(128)S(1)} %get-tuple-element.40.s, bf16[1040,768]{1,0:T(8,128)(2,1)S(1)} %get-tuple-element.56.x_ref, bf16[1040,768]{1,0:T(8,128)(2,1)S(1)} %collective-permute-done.2.sib_ref, ...), custom_call_target="tpu_custom_call", output_to_operand_aliasing={{0}: (4, {}), {1}: (5, {})} | custom-call | flops 17250000896 | bytes 1024 | tf_op jit(solution)/shard_map/pallas_call | solution.py:421
  23.7 4.1 %collective-permute-done.1.q_ref.qb_ref = bf16[256,768]{1,0:T(8,128)(2,1)S(1)} collective-permute-done((bf16[256,768]{1,0:T(8,128)(2,1)S(1)}, bf16[256,768]{1,0:T(8,128)(2,1)S(1)}, u32[]{:S(2)}, u32[]{:S(2)}) %collective-permute-start.1) | collective-permute-done | bytes 393248 | tf_op jit(solution)/shard_map/ppermute | solution.py:451
  27.9 0.6 %shard_map.65 = bf16[272,768]{1,0:T(8,128)(2,1)S(1)} custom-call(s32[8]{0:T(128)S(1)} %get-tuple-element.40.s, bf16[256,768]{1,0:T(8,128)(2,1)S(1)} %collective-permute-done.1.q_ref.qb_ref, bf16[1040,768]{1,0:T(8,128)(2,1)S(1)} %get-tuple-element.56.x_ref, bf16[1040,768]{1,0:T(8,128)(2,1)S(1)} %collective-permute-done.2.sib_ref, ...), custom_call_target="tpu_custom_call", output_to_operand_aliasing={{}: (5, {})} | custom-call | flops 11500000256 | bytes 1024 | tf_op jit(solution)/shard_map/pallas_call | solution.py:421
  28.4 1.9 %collective-permute-start.3 = (bf16[272,768]{1,0:T(8,128)(2,1)S(1)}, bf16[272,768]{1,0:T(8,128)(2,1)S(1)}, u32[]{:S(2)}, u32[]{:S(2)}) collective-permute-start(bf16[272,768]{1,0:T(8,128)(2,1)S(1)} %shard_map.65), channel_id=1, source_target_pairs={{1,2},{3,4},{5,6},{7,8},{9,10},{11,12},{13,14},{2,1},{4,3},{6,5},{... | collective-permute-start | bytes 1253384 | tf_op jit(solution)/shard_map/ppermute | solution.py:451
  30.3 0.1 collective-permute-start.5
  30.4 0.5 %collective-permute-start.6 = (bf16[256,768]{1,0:T(8,128)(2,1)S(1)}, bf16[256,768]{1,0:T(8,128)(2,1)S(1)}, u32[]{:S(2)}, u32[]{:S(2)}) collective-permute-start(bf16[256,768]{1,0:T(8,128)(2,1)S(1)} %collective-permute-done.1.q_ref.qb_ref), channel_id=1, source_target_pairs={{0,1},{1,0},{2,3},{3,2},{4,5},{5,4},{6,7},{7,6},{8,9},{9,8},{10,11... | collective-permute-start | bytes 1179656 | tf_op jit(solution)/shard_map/ppermute | solution.py:454
  30.9 1.7 %shard_map.66 = (s32[10]{0:T(128)S(4)}, f32[1024,128]{1,0:T(8,128)S(1)}, f32[1024,768]{1,0:T(8,128)S(1)}) custom-call(s32[8]{0:T(128)S(1)} %get-tuple-element.40.s, bf16[1040,768]{1,0:T(8,128)(2,1)S(1)} %get-tuple-element.56.x_ref, bf16[256,768]{1,0:T(8,128)(2,1)S(1)} %collective-permute-done.q_ref.qa_ref, ...), custom_call_target="tpu_custom_call", output_to_operand_aliasing={{1}: (4, {}), {2}: (5, {})} | custom-call | flops 17250000896 | bytes 1024 | tf_op jit(solution)/shard_map/pallas_call | solution.py:421
  32.7 0.0 collective-permute-done.6.fb_ref
  32.7 0.7 %shard_map.67 = (f32[1024,128]{1,0:T(8,128)S(1)}, f32[1024,768]{1,0:T(8,128)S(1)}) custom-call(s32[8]{0:T(128)S(1)} %get-tuple-element.40.s, bf16[1040,768]{1,0:T(8,128)(2,1)S(1)} %get-tuple-element.56.x_ref, bf16[1040,768]{1,0:T(8,128)(2,1)S(1)} %collective-permute-done.2.sib_ref, ...), custom_call_target="tpu_custom_call", output_to_operand_aliasing={{0}: (5, {}), {1}: (6, {})} | custom-call | flops 17250000896 | bytes 1024 | tf_op jit(solution)/shard_map/pallas_call | solution.py:421
  33.4 3.2 %collective-permute-done.4.q_ref = bf16[256,768]{1,0:T(8,128)(2,1)S(1)} collective-permute-done((bf16[256,768]{1,0:T(8,128)(2,1)S(1)}, bf16[256,768]{1,0:T(8,128)(2,1)S(1)}, u32[]{:S(2)}, u32[]{:S(2)}) %collective-permute-start.4) | collective-permute-done | bytes 393248 | tf_op jit(solution)/shard_map/ppermute | solution.py:451
  36.5 1.2 %shard_map.68 = (f32[8,512]{1,0:T(8,128)S(1)}, f32[8,128]{1,0:T(8,128)}, bf16[1024,768]{1,0:T(8,128)(2,1)}, f32[1024,128]{1,0:T(8,128)S(1)}, f32[1024,768]{1,0:T(8,128)S(1)}) custom-call(s32[10]{0:T(128)S(4)} %get-tuple-element.61.s, bf16[1040,768]{1,0:T(8,128)(2,1)S(1)} %get-tuple-element.56.x_ref, ...), custom_call_target="tpu_custom_call", output_to_operand_aliasing={{3}: (3, {}), {4}: (4, {})} | custom-call | flops 5750000128 | bytes 1024 | tf_op jit(solution)/shard_map/pallas_call | solution.py:421
  37.7 3.3 %collective-permute-done.3.q_ref = bf16[272,768]{1,0:T(8,128)(2,1)S(1)} collective-permute-done((bf16[272,768]{1,0:T(8,128)(2,1)S(1)}, bf16[272,768]{1,0:T(8,128)(2,1)S(1)}, u32[]{:S(2)}, u32[]{:S(2)}) %collective-permute-start.3) | collective-permute-done | bytes 417824 | tf_op jit(solution)/shard_map/ppermute | solution.py:451
  41.0 2.1 %shard_map.69 = (f32[8,128]{1,0:T(8,128)}, bf16[1024,768]{1,0:T(8,128)(2,1)}) custom-call(s32[10]{0:T(128)S(4)} %get-tuple-element.61.s, bf16[1040,768]{1,0:T(8,128)(2,1)S(1)} %get-tuple-element.56.x_ref, bf16[272,768]{1,0:T(8,128)(2,1)S(1)} %collective-permute-done.3.q_ref, ...), custom_call_target="tpu_custom_call", output_to_operand_aliasing={{0}: (6, {}), {1}: (7, {})} | custom-call | flops 5750000128 | bytes 1024 | tf_op jit(solution)/shard_map/pallas_call | solution.py:421
  (1 shorter events, 0.0 us)
Async XLA Ops:
  1.8 13.4 %collective-permute-start = (bf16[256,768]{1,0:T(8,128)(2,1)S(1)}, bf16[256,768]{1,0:T(8,128)(2,1)S(1)}, u32[]{:S(2)}, u32[]{:S(2)}) collective-permute-start(bf16[256,768]{1,0:T(8,128)(2,1)S(1)} %shard_map.59), channel_id=1, source_target_pairs={{1,2},{3,4},{5,6},{7,8},{9,10},{11,12},{13,14},{2,1},{4,3},{6,5},{... | collective-permute-start | bytes 1179656 | tf_op jit(solution)/shard_map/ppermute | solution.py:451
  8.4 6.8 %collective-permute-start.2 = (bf16[1040,768]{1,0:T(8,128)(2,1)S(1)}, bf16[1040,768]{1,0:T(8,128)(2,1)S(1)}, u32[]{:S(2)}, u32[]{:S(2)}) collective-permute-start(bf16[1040,768]{1,0:T(8,128)(2,1)S(1)} %get-tuple-element.56.x_ref), channel_id=1, source_target_pairs={{0,1},{1,0},{2,3},{3,2},{4,5},{5,4},{6,7},{7,6},{8,9},{9,8},{10,11... | collective-permute-start | bytes 4792328 | tf_op jit(solution)/shard_map/ppermute | solution.py:454
  10.2 17.6 %collective-permute-start.1 = (bf16[256,768]{1,0:T(8,128)(2,1)S(1)}, bf16[256,768]{1,0:T(8,128)(2,1)S(1)}, u32[]{:S(2)}, u32[]{:S(2)}) collective-permute-start(bf16[256,768]{1,0:T(8,128)(2,1)S(1)} %get-tuple-element.45), channel_id=1, source_target_pairs={{1,2},{3,4},{5,6},{7,8},{9,10},{11,12},{13,14},{2,1},{4,3},{6,5},{... | collective-permute-start | bytes 1179656 | tf_op jit(solution)/shard_map/ppermute | solution.py:451
  15.8 20.8 %collective-permute-start.4 = (bf16[256,768]{1,0:T(8,128)(2,1)S(1)}, bf16[256,768]{1,0:T(8,128)(2,1)S(1)}, u32[]{:S(2)}, u32[]{:S(2)}) collective-permute-start(bf16[256,768]{1,0:T(8,128)(2,1)S(1)} %get-tuple-element.51), channel_id=1, source_target_pairs={{1,2},{3,4},{5,6},{7,8},{9,10},{11,12},{13,14},{2,1},{4,3},{6,5},{... | collective-permute-start | bytes 1179656 | tf_op jit(solution)/shard_map/ppermute | solution.py:451
  28.4 12.6 %collective-permute-start.3 = (bf16[272,768]{1,0:T(8,128)(2,1)S(1)}, bf16[272,768]{1,0:T(8,128)(2,1)S(1)}, u32[]{:S(2)}, u32[]{:S(2)}) collective-permute-start(bf16[272,768]{1,0:T(8,128)(2,1)S(1)} %shard_map.65), channel_id=1, source_target_pairs={{1,2},{3,4},{5,6},{7,8},{9,10},{11,12},{13,14},{2,1},{4,3},{6,5},{... | collective-permute-start | bytes 1253384 | tf_op jit(solution)/shard_map/ppermute | solution.py:451
  30.3 2.3 %collective-permute-start.5 = (bf16[256,768]{1,0:T(8,128)(2,1)S(1)}, bf16[256,768]{1,0:T(8,128)(2,1)S(1)}, u32[]{:S(2)}, u32[]{:S(2)}) collective-permute-start(bf16[256,768]{1,0:T(8,128)(2,1)S(1)} %collective-permute-done.q_ref.qa_ref), channel_id=1, source_target_pairs={{0,1},{1,0},{2,3},{3,2},{4,5},{5,4},{6,7},{7,6},{8,9},{9,8},{10,11... | collective-permute-start | bytes 1179656 | tf_op jit(solution)/shard_map/ppermute | solution.py:454
  30.4 2.3 %collective-permute-start.6 = (bf16[256,768]{1,0:T(8,128)(2,1)S(1)}, bf16[256,768]{1,0:T(8,128)(2,1)S(1)}, u32[]{:S(2)}, u32[]{:S(2)}) collective-permute-start(bf16[256,768]{1,0:T(8,128)(2,1)S(1)} %collective-permute-done.1.q_ref.qb_ref), channel_id=1, source_target_pairs={{0,1},{1,0},{2,3},{3,2},{4,5},{5,4},{6,7},{7,6},{8,9},{9,8},{10,11... | collective-permute-start | bytes 1179656 | tf_op jit(solution)/shard_map/ppermute | solution.py:454

commit v4 on v3

--- a/solution.py
+++ b/solution.py
@@ -262,20 +262,19 @@
         partial_sums(s, q_ref, x_ref, sib_ref, out_ref, dens_ref)
 
 
-def fourth_kernel(s, q_ref, x_ref, sib_ref, dens_a_ref, out_in, out_ref, dens_ref):
+def fourth_kernel(s, q_ref, x_ref, sib_ref, dens_a_ref, out_in, out_ref, tile_ref, dens_ref):
     @pl.when(sums_go(s))
     def _():
         partial_sums(s, q_ref, x_ref, sib_ref, out_ref, dens_ref)
-        width = out_ref.shape[1]
         both = [along_lanes(dens_a_ref[...]), along_lanes(dens_ref[...])]
-        row = jnp.concatenate(both + [jnp.zeros((1, width - BLOCK), jnp.float32)], axis=1)
-        place = iota((TILE, width), 0)
-        tile = jnp.zeros((TILE, width), jnp.float32)
+        row = jnp.concatenate(both, axis=1)
+        place = iota(tile_ref.shape, 0)
+        tile = jnp.zeros(tile_ref.shape, jnp.float32)
         for piece in range(3):
             rounded = row.astype(jnp.bfloat16).astype(jnp.float32)
             tile = jnp.where(place == piece, rounded, tile)
             row = row - rounded
-        out_ref[HALF:, :] = tile.astype(jnp.bfloat16)
+        tile_ref[...] = tile.astype(jnp.bfloat16)
 
 
 def outer_kernel(s, x_ref, qa_ref, qb_ref, dens_in, acc_in, came, dens_ref, acc_ref):
@@ -361,7 +360,7 @@
 
 
 def last_kernel(
-    s, x_ref, q_ref, lanes_ref, dens_ref, acc_ref, log_in, out_in, log_out, out_ref,
+    s, x_ref, q_ref, tile_ref, lanes_ref, dens_ref, acc_ref, log_in, out_in, log_out, out_ref,
     rows_ref, log_ref, sems
 ):
     log_copy = pltpu.make_async_copy(log_ref, log_out, sems.at[4])
@@ -404,9 +403,9 @@
         rows_ref[rows, :] = finished(sums, HALF, real)
         copy = pltpu.make_async_copy(rows_ref.at[rows, :], out_ref.at[rows, :], sems.at[0])
         copy.start()
-        tile = q_ref[HALF:, :].astype(jnp.float32)
-        pieces = jnp.where(iota(tile.shape, 0) < 3, tile, 0.0)
-        more = jnp.sum(pieces, axis=0, keepdims=True)[:, 0:BLOCK]
+        pieces = tile_ref[...].astype(jnp.float32)
+        pieces = jnp.where(iota(pieces.shape, 0) < 3, pieces, 0.0)
+        more = jnp.sum(pieces, axis=0, keepdims=True)
         for b in range(2):
             density = lanes_ref[b : b + 1, :] + jnp.where(s[PAR] == b, more, 0.0)
             put_logs(log_ref, b, logs_of(density, s[V0 + b]))
@@ -492,7 +491,7 @@
         13.0,
         "svvv",
         (table, x, dens, acc),
-        [bf16(HALF), bf16(HALF + TILE)] + state,
+        [bf16(HALF), bf16(HALF)] + state,
         aliases={2: 2, 3: 3},
     )
     third, dens_a = call(
@@ -508,17 +507,18 @@
     dens, acc = call(
         middle_kernel, 15.0, "svvvvv", (table, x, sib, qa, dens, acc), state, aliases={4: 0, 5: 1}
     )
-    (fourth,) = call(
+    fourth, tile = call(
         fourth_kernel,
         10.0,
         "svvvvv",
         (table, qb, after(x, acc), sib, dens_a, fourth),
-        [bf16(HALF + TILE)],
+        [bf16(HALF), jax.ShapeDtypeStruct((TILE, BLOCK), jnp.bfloat16)],
         aliases={5: 0},
         scratch=(pltpu.VMEM((HALF, LANES), jnp.float32),),
     )
     dens, acc, fourth = lax.optimization_barrier((dens, acc, fourth))
     qd = over_edge(fourth)
+    qe = over_edge(after(tile, fourth))
     fa = to_sibling(after(qa, fourth))
     fb = to_sibling(after(qb, fourth))
     came, dens, acc = call(
@@ -552,11 +552,11 @@
     logs, sums = call(
         last_kernel,
         5.0,
-        "svvvvvhh",
-        (came, x, qd, lanes, dens, acc, logs, sums),
+        "svvvvvvhh",
+        (came, x, qd, qe, lanes, dens, acc, logs, sums),
         [log_shape, bf16(2 * BLOCK)],
         "hh",
-        aliases={6: 0, 7: 1},
+        aliases={7: 0, 8: 1},
         scratch=(vmem(2 * BLOCK), pltpu.VMEM(log_shape.shape, jnp.float32), dma(5)),
     )
     return logs.reshape(-1), sums

time: 42.9 us -> 42.8 us (level)
  the two profiles are of different devices: /device:TPU:25 before, /device:TPU:19 now
where the time goes in v4:
time: 42.8 us; the launch traced here: 43.1 us
  starting transfers between devices  20.3 us (47%)
  Pallas kernels  17.1 us (40%)
  waiting for transfers between devices  4.06 us (9%)
  between operations  1.58 us (4%)
    pallas_call x11, Pallas kernels, call(): pl.pallas_call(kernel, in_specs=[spaces[c] for c in in_spaces], out_specs...  17.1 us
    ppermute x5, starting transfers between devices, over_edge(): return lax.ppermute(block, 'cluster', edges)  17 us
    ppermute x5, waiting for transfers between devices, over_edge(): return lax.ppermute(block, 'cluster', edges)  3.97 us
    ppermute x3, starting transfers between devices, to_sibling(): return lax.ppermute(block, 'cluster', inchip)  3.35 us
  transfers between devices with their start and end apart: 8, of which 4 were waited for; matrix products, arithmetic and copies ran while one was open for 0% of the time, Pallas kernels for 32%

profile of v4, /device:TPU:19, one launch (start us, length us, event | category | flops | bytes accessed | tf_op | source)
XLA Modules:
  0.0 43.1 jit_solution(17415954906792987021)
XLA Ops:
  0.6 1.2 %shard_map.59 = bf16[256,768]{1,0:T(8,128)(2,1)S(1)} custom-call(s32[1]{0:T(128)} %bitcast.idx_ref, s32[8,128]{1,0:T(8,128)} %bitcast.4, bf16[1024,768]{1,0:T(8,128)(2,1)} %embed_ref.3), custom_call_target="tpu_custom_call" | custom-call | flops 6899999744 | bytes 1024 | tf_op jit(solution)/shard_map/pallas_call | solution.py:420
  1.8 3.7 %collective-permute-start = (bf16[256,768]{1,0:T(8,128)(2,1)S(1)}, bf16[256,768]{1,0:T(8,128)(2,1)S(1)}, u32[]{:S(2)}, u32[]{:S(2)}) collective-permute-start(bf16[256,768]{1,0:T(8,128)(2,1)S(1)} %shard_map.59), channel_id=1, source_target_pairs={{1,2},{3,4},{5,6},{7,8},{9,10},{11,12},{13,14},{2,1},{4,3},{6,5},{... | collective-permute-start | bytes 1179656 | tf_op jit(solution)/shard_map/ppermute | solution.py:450
  6.2 2.2 %shard_map.60 = (s32[8]{0:T(128)S(1)}, bf16[1040,768]{1,0:T(8,128)(2,1)S(1)}, bf16[256,768]{1,0:T(8,128)(2,1)S(1)}) custom-call(s32[1]{0:T(128)} %bitcast.idx_ref, s32[2,7]{1,0:T(2,128)} %bitcast.6, s32[1]{0:T(128)S(6)} %copy.34.count_ref, s32[8,128]{1,0:T(8,128)} %bitcast.5, bf16[1024,768]{1,0:T(8,128)(2,1)} %embed_ref.3), custom_call_target="tpu_custom_call" | custom-call | flops 16099999744 | bytes 1024 | tf_op jit(solution)/shard_map/pallas_call | solution.py:420
  8.4 0.1 collective-permute-start.2
  8.5 1.7 %shard_map.61 = (f32[1024,128]{1,0:T(8,128)S(1)}, f32[1024,768]{1,0:T(8,128)S(1)}) custom-call(s32[8]{0:T(128)S(1)} %get-tuple-element.43.s, bf16[1040,768]{1,0:T(8,128)(2,1)S(1)} %get-tuple-element.59.x_ref), custom_call_target="tpu_custom_call" | custom-call | flops 34500001792 | bytes 1024 | tf_op jit(solution)/shard_map/pallas_call | solution.py:420
  10.2 3.5 %collective-permute-start.1 = (bf16[256,768]{1,0:T(8,128)(2,1)S(1)}, bf16[256,768]{1,0:T(8,128)(2,1)S(1)}, u32[]{:S(2)}, u32[]{:S(2)}) collective-permute-start(bf16[256,768]{1,0:T(8,128)(2,1)S(1)} %get-tuple-element.48), channel_id=1, source_target_pairs={{1,2},{3,4},{5,6},{7,8},{9,10},{11,12},{13,14},{2,1},{4,3},{6,5},{... | collective-permute-start | bytes 1179656 | tf_op jit(solution)/shard_map/ppermute | solution.py:450
  13.7 1.9 %shard_map.62 = (bf16[256,768]{1,0:T(8,128)(2,1)S(1)}, bf16[256,768]{1,0:T(8,128)(2,1)S(1)}, f32[1024,128]{1,0:T(8,128)S(1)}, f32[1024,768]{1,0:T(8,128)S(1)}) custom-call(s32[8]{0:T(128)S(1)} %get-tuple-element.43.s, bf16[1040,768]{1,0:T(8,128)(2,1)S(1)} %get-tuple-element.59.x_ref, ...), custom_call_target="tpu_custom_call", output_to_operand_aliasing={{2}: (2, {}), {3}: (3, {})} | custom-call | flops 14949999616 | bytes 1024 | tf_op jit(solution)/shard_map/pallas_call | solution.py:420
  15.6 0.0 collective-permute-done.2.sib_ref
  15.6 0.6 %shard_map.63 = (bf16[256,768]{1,0:T(8,128)(2,1)S(1)}, f32[256,128]{1,0:T(8,128)S(1)}) custom-call(s32[8]{0:T(128)S(1)} %get-tuple-element.43.s, bf16[256,768]{1,0:T(8,128)(2,1)S(1)} %collective-permute-done.q_ref.qa_ref, bf16[1040,768]{1,0:T(8,128)(2,1)S(1)} %get-tuple-element.59.x_ref, ...), custom_call_target="tpu_custom_call", output_to_operand_aliasing={{0}: (4, {})} | custom-call | flops 11500000256 | bytes 1024 | tf_op jit(solution)/shard_map/pallas_call | solution.py:420
  16.2 4.2 %collective-permute-start.5 = (bf16[256,768]{1,0:T(8,128)(2,1)S(1)}, bf16[256,768]{1,0:T(8,128)(2,1)S(1)}, u32[]{:S(2)}, u32[]{:S(2)}) collective-permute-start(bf16[256,768]{1,0:T(8,128)(2,1)S(1)} %get-tuple-element.54), channel_id=1, source_target_pairs={{1,2},{3,4},{5,6},{7,8},{9,10},{11,12},{13,14},{2,1},{4,3},{6,5},{... | collective-permute-start | bytes 1179656 | tf_op jit(solution)/shard_map/ppermute | solution.py:450
  20.4 3.4 %shard_map.64 = (f32[1024,128]{1,0:T(8,128)S(1)}, f32[1024,768]{1,0:T(8,128)S(1)}) custom-call(s32[8]{0:T(128)S(1)} %get-tuple-element.43.s, bf16[1040,768]{1,0:T(8,128)(2,1)S(1)} %get-tuple-element.59.x_ref, bf16[1040,768]{1,0:T(8,128)(2,1)S(1)} %collective-permute-done.2.sib_ref, ...), custom_call_target="tpu_custom_call", output_to_operand_aliasing={{0}: (4, {}), {1}: (5, {})} | custom-call | flops 17250000896 | bytes 1024 | tf_op jit(solution)/shard_map/pallas_call | solution.py:420
  23.8 0.2 collective-permute-done.1.q_ref.qb_ref
  23.9 0.6 %shard_map.65 = (bf16[256,768]{1,0:T(8,128)(2,1)S(1)}, bf16[16,512]{1,0:T(8,128)(2,1)S(1)}) custom-call(s32[8]{0:T(128)S(1)} %get-tuple-element.43.s, bf16[256,768]{1,0:T(8,128)(2,1)S(1)} %collective-permute-done.1.q_ref.qb_ref, bf16[1040,768]{1,0:T(8,128)(2,1)S(1)} %get-tuple-element.59.x_ref, ...), custom_call_target="tpu_custom_call", output_to_operand_aliasing={{0}: (5, {})} | custom-call | flops 11500000256 | bytes 1024 | tf_op jit(solution)/shard_map/pallas_call | solution.py:420
  24.5 3.3 %collective-permute-start.3 = (bf16[256,768]{1,0:T(8,128)(2,1)S(1)}, bf16[256,768]{1,0:T(8,128)(2,1)S(1)}, u32[]{:S(2)}, u32[]{:S(2)}) collective-permute-start(bf16[256,768]{1,0:T(8,128)(2,1)S(1)} %get-tuple-element.66), channel_id=1, source_target_pairs={{1,2},{3,4},{5,6},{7,8},{9,10},{11,12},{13,14},{2,1},{4,3},{6,5},{... | collective-permute-start | bytes 1179656 | tf_op jit(solution)/shard_map/ppermute | solution.py:450
  27.9 2.2 %collective-permute-start.4 = (bf16[16,512]{1,0:T(8,128)(2,1)S(1)}, bf16[16,512]{1,0:T(8,128)(2,1)S(1)}, u32[]{:S(2)}, u32[]{:S(2)}) collective-permute-start(bf16[16,512]{1,0:T(8,128)(2,1)S(1)} %get-tuple-element.68), channel_id=1, source_target_pairs={{1,2},{3,4},{5,6},{7,8},{9,10},{11,12},{13,14},{2,1},{4,3},{6,5},{... | collective-permute-start | bytes 49160 | tf_op jit(solution)/shard_map/ppermute | solution.py:450
  30.1 3.2 %collective-permute-start.6 = (bf16[256,768]{1,0:T(8,128)(2,1)S(1)}, bf16[256,768]{1,0:T(8,128)(2,1)S(1)}, u32[]{:S(2)}, u32[]{:S(2)}) collective-permute-start(bf16[256,768]{1,0:T(8,128)(2,1)S(1)} %collective-permute-done.q_ref.qa_ref), channel_id=1, source_target_pairs={{0,1},{1,0},{2,3},{3,2},{4,5},{5,4},{6,7},{7,6},{8,9},{9,8},{10,11... | collective-permute-start | bytes 1179656 | tf_op jit(solution)/shard_map/ppermute | solution.py:453
  33.3 0.1 collective-permute-start.7
  33.4 1.7 %shard_map.66 = (s32[10]{0:T(128)S(4)}, f32[1024,128]{1,0:T(8,128)S(1)}, f32[1024,768]{1,0:T(8,128)S(1)}) custom-call(s32[8]{0:T(128)S(1)} %get-tuple-element.43.s, bf16[1040,768]{1,0:T(8,128)(2,1)S(1)} %get-tuple-element.59.x_ref, bf16[256,768]{1,0:T(8,128)(2,1)S(1)} %collective-permute-done.q_ref.qa_ref, ...), custom_call_target="tpu_custom_call", output_to_operand_aliasing={{1}: (4, {}), {2}: (5, {})} | custom-call | flops 17250000896 | bytes 1024 | tf_op jit(solution)/shard_map/pallas_call | solution.py:420
  35.1 0.1 collective-permute-done.7.fb_ref
  35.2 0.7 %shard_map.67 = (f32[1024,128]{1,0:T(8,128)S(1)}, f32[1024,768]{1,0:T(8,128)S(1)}) custom-call(s32[8]{0:T(128)S(1)} %get-tuple-element.43.s, bf16[1040,768]{1,0:T(8,128)(2,1)S(1)} %get-tuple-element.59.x_ref, bf16[1040,768]{1,0:T(8,128)(2,1)S(1)} %collective-permute-done.2.sib_ref, ...), custom_call_target="tpu_custom_call", output_to_operand_aliasing={{0}: (5, {}), {1}: (6, {})} | custom-call | flops 17250000896 | bytes 1024 | tf_op jit(solution)/shard_map/pallas_call | solution.py:420
  35.9 0.7 %collective-permute-done.5.q_ref = bf16[256,768]{1,0:T(8,128)(2,1)S(1)} collective-permute-done((bf16[256,768]{1,0:T(8,128)(2,1)S(1)}, bf16[256,768]{1,0:T(8,128)(2,1)S(1)}, u32[]{:S(2)}, u32[]{:S(2)}) %collective-permute-start.5) | collective-permute-done | bytes 393248 | tf_op jit(solution)/shard_map/ppermute | solution.py:450
  36.6 1.2 %shard_map.68 = (f32[8,512]{1,0:T(8,128)S(1)}, f32[8,128]{1,0:T(8,128)}, bf16[1024,768]{1,0:T(8,128)(2,1)}, f32[1024,128]{1,0:T(8,128)S(1)}, f32[1024,768]{1,0:T(8,128)S(1)}) custom-call(s32[10]{0:T(128)S(4)} %get-tuple-element.65.s, bf16[1040,768]{1,0:T(8,128)(2,1)S(1)} %get-tuple-element.59.x_ref, ...), custom_call_target="tpu_custom_call", output_to_operand_aliasing={{3}: (3, {}), {4}: (4, {})} | custom-call | flops 5750000128 | bytes 1024 | tf_op jit(solution)/shard_map/pallas_call | solution.py:420
  37.8 3.1 %collective-permute-done.4.tile_ref = bf16[16,512]{1,0:T(8,128)(2,1)S(1)} collective-permute-done((bf16[16,512]{1,0:T(8,128)(2,1)S(1)}, bf16[16,512]{1,0:T(8,128)(2,1)S(1)}, u32[]{:S(2)}, u32[]{:S(2)}) %collective-permute-start.4) | collective-permute-done | bytes 16416 | tf_op jit(solution)/shard_map/ppermute | solution.py:450
  40.8 2.1 %shard_map.69 = (f32[8,128]{1,0:T(8,128)}, bf16[1024,768]{1,0:T(8,128)(2,1)}) custom-call(s32[10]{0:T(128)S(4)} %get-tuple-element.65.s, bf16[1040,768]{1,0:T(8,128)(2,1)S(1)} %get-tuple-element.59.x_ref, bf16[256,768]{1,0:T(8,128)(2,1)S(1)} %collective-permute-done.3.q_ref, ...), custom_call_target="tpu_custom_call", output_to_operand_aliasing={{0}: (7, {}), {1}: (8, {})} | custom-call | flops 5750000128 | bytes 1024 | tf_op jit(solution)/shard_map/pallas_call | solution.py:420
  (3 shorter events, 0.0 us)
Async XLA Ops:
  1.8 13.8 %collective-permute-start = (bf16[256,768]{1,0:T(8,128)(2,1)S(1)}, bf16[256,768]{1,0:T(8,128)(2,1)S(1)}, u32[]{:S(2)}, u32[]{:S(2)}) collective-permute-start(bf16[256,768]{1,0:T(8,128)(2,1)S(1)} %shard_map.59), channel_id=1, source_target_pairs={{1,2},{3,4},{5,6},{7,8},{9,10},{11,12},{13,14},{2,1},{4,3},{6,5},{... | collective-permute-start | bytes 1179656 | tf_op jit(solution)/shard_map/ppermute | solution.py:450
  8.4 7.2 %collective-permute-start.2 = (bf16[1040,768]{1,0:T(8,128)(2,1)S(1)}, bf16[1040,768]{1,0:T(8,128)(2,1)S(1)}, u32[]{:S(2)}, u32[]{:S(2)}) collective-permute-start(bf16[1040,768]{1,0:T(8,128)(2,1)S(1)} %get-tuple-element.59.x_ref), channel_id=1, source_target_pairs={{0,1},{1,0},{2,3},{3,2},{4,5},{5,4},{6,7},{7,6},{8,9},{9,8},{10,11... | collective-permute-start | bytes 4792328 | tf_op jit(solution)/shard_map/ppermute | solution.py:453
  10.2 13.7 %collective-permute-start.1 = (bf16[256,768]{1,0:T(8,128)(2,1)S(1)}, bf16[256,768]{1,0:T(8,128)(2,1)S(1)}, u32[]{:S(2)}, u32[]{:S(2)}) collective-permute-start(bf16[256,768]{1,0:T(8,128)(2,1)S(1)} %get-tuple-element.48), channel_id=1, source_target_pairs={{1,2},{3,4},{5,6},{7,8},{9,10},{11,12},{13,14},{2,1},{4,3},{6,5},{... | collective-permute-start | bytes 1179656 | tf_op jit(solution)/shard_map/ppermute | solution.py:450
  16.2 20.4 %collective-permute-start.5 = (bf16[256,768]{1,0:T(8,128)(2,1)S(1)}, bf16[256,768]{1,0:T(8,128)(2,1)S(1)}, u32[]{:S(2)}, u32[]{:S(2)}) collective-permute-start(bf16[256,768]{1,0:T(8,128)(2,1)S(1)} %get-tuple-element.54), channel_id=1, source_target_pairs={{1,2},{3,4},{5,6},{7,8},{9,10},{11,12},{13,14},{2,1},{4,3},{6,5},{... | collective-permute-start | bytes 1179656 | tf_op jit(solution)/shard_map/ppermute | solution.py:450
  24.5 16.4 %collective-permute-start.3 = (bf16[256,768]{1,0:T(8,128)(2,1)S(1)}, bf16[256,768]{1,0:T(8,128)(2,1)S(1)}, u32[]{:S(2)}, u32[]{:S(2)}) collective-permute-start(bf16[256,768]{1,0:T(8,128)(2,1)S(1)} %get-tuple-element.66), channel_id=1, source_target_pairs={{1,2},{3,4},{5,6},{7,8},{9,10},{11,12},{13,14},{2,1},{4,3},{6,5},{... | collective-permute-start | bytes 1179656 | tf_op jit(solution)/shard_map/ppermute | solution.py:450
  27.9 13.0 %collective-permute-start.4 = (bf16[16,512]{1,0:T(8,128)(2,1)S(1)}, bf16[16,512]{1,0:T(8,128)(2,1)S(1)}, u32[]{:S(2)}, u32[]{:S(2)}) collective-permute-start(bf16[16,512]{1,0:T(8,128)(2,1)S(1)} %get-tuple-element.68), channel_id=1, source_target_pairs={{1,2},{3,4},{5,6},{7,8},{9,10},{11,12},{13,14},{2,1},{4,3},{6,5},{... | collective-permute-start | bytes 49160 | tf_op jit(solution)/shard_map/ppermute | solution.py:450
  30.1 5.0 %collective-permute-start.6 = (bf16[256,768]{1,0:T(8,128)(2,1)S(1)}, bf16[256,768]{1,0:T(8,128)(2,1)S(1)}, u32[]{:S(2)}, u32[]{:S(2)}) collective-permute-start(bf16[256,768]{1,0:T(8,128)(2,1)S(1)} %collective-permute-done.q_ref.qa_ref), channel_id=1, source_target_pairs={{0,1},{1,0},{2,3},{3,2},{4,5},{5,4},{6,7},{7,6},{8,9},{9,8},{10,11... | collective-permute-start | bytes 1179656 | tf_op jit(solution)/shard_map/ppermute | solution.py:453
  33.3 1.9 %collective-permute-start.7 = (bf16[256,768]{1,0:T(8,128)(2,1)S(1)}, bf16[256,768]{1,0:T(8,128)(2,1)S(1)}, u32[]{:S(2)}, u32[]{:S(2)}) collective-permute-start(bf16[256,768]{1,0:T(8,128)(2,1)S(1)} %collective-permute-done.1.q_ref.qb_ref), channel_id=1, source_target_pairs={{0,1},{1,0},{2,3},{3,2},{4,5},{5,4},{6,7},{7,6},{8,9},{9,8},{10,11... | collective-permute-start | bytes 1179656 | tf_op jit(solution)/shard_map/ppermute | solution.py:453

commit v5 on v4

--- a/solution.py
+++ b/solution.py
@@ -369,28 +369,38 @@
     def _():
         count = real_rows(q_ref, 0, HALF)
         right = q_ref[0:HALF, :]
+        counts = [jnp.where(s[PAR] == b, count, count * s[E0]) for b in range(2)]
+        copies = []
+
+        def finish(start, rows, kern):
+            place = pl.ds(start, rows)
+            sums = acc_ref[place, :] + jnp.dot(
+                kern.astype(jnp.bfloat16), right, preferred_element_type=jnp.float32
+            )
+            rows_ref[place, :] = finished(sums, start % BLOCK, s[V0 + start // BLOCK])
+            copy = pltpu.make_async_copy(
+                rows_ref.at[place, :], out_ref.at[place, :], sems.at[start // HALF]
+            )
+            copy.start()
+            copies.append(copy)
+
+        def log_block(b, density):
+            put_logs(log_ref, b, logs_of(along_lanes(density), s[V0 + b]))
+
         kerns = []
+        for t in range(4):
+            place = pl.ds(t * HALF, HALF)
+            kerns.append(kernel_tile(x_ref[place, :], right, counts[t // 2]))
+            if t:
+                finish((t - 1) * HALF, HALF, kerns[t - 1])
         for b in range(2):
-            left = x_ref[b * BLOCK : (b + 1) * BLOCK, :]
-            kerns.append(kernel_tile(left, right, jnp.where(s[PAR] == b, count, count * s[E0])))
-        copies = []
-        for b in range(2):
-            for half in range(2):
-                rows = pl.ds(b * BLOCK + half * HALF, HALF)
-                kern = kerns[b][half * HALF : (half + 1) * HALF].astype(jnp.bfloat16)
-                sums = acc_ref[rows, :] + jnp.dot(kern, right, preferred_element_type=jnp.float32)
-                rows_ref[rows, :] = finished(sums, half * HALF, s[V0 + b])
-                copy = pltpu.make_async_copy(
-                    rows_ref.at[rows, :], out_ref.at[rows, :], sems.at[2 * b + half]
-                )
-                copy.start()
-                copies.append(copy)
-            if b == 0:
-                for c in range(2):
-                    density = dens_ref[c * BLOCK : (c + 1) * BLOCK, :] + folded(kerns[c])
-                    put_logs(log_ref, c, logs_of(along_lanes(density), s[V0 + c]))
-                log_copy.start()
-                copies.append(log_copy)
+            density = [
+                dens_ref[pl.ds(t * HALF, HALF), :] + folded(kerns[t]) for t in (2 * b, 2 * b + 1)
+            ]
+            log_block(b, jnp.concatenate(density, axis=0))
+        log_copy.start()
+        copies.append(log_copy)
+        finish(3 * HALF, HALF, kerns[3])
         for copy in copies:
             copy.wait()
 

time: 42.8 us -> 43.5 us (1.016)
  the two profiles are of different devices: /device:TPU:19 before, /device:TPU:20 now
where the time goes in v5:
time: 43.5 us; the launch traced here: 43 us
  Pallas kernels  22.6 us (52%)
  starting transfers between devices  16.5 us (38%)
  waiting for transfers between devices  2.36 us (5%)
  between operations  1.59 us (4%)
    pallas_call x11, Pallas kernels, call(): pl.pallas_call(kernel, in_specs=[spaces[c] for c in in_spaces], out_specs...  22.6 us
    ppermute x5, starting transfers between devices, over_edge(): return lax.ppermute(block, 'cluster', edges)  11.4 us
    ppermute x3, starting transfers between devices, to_sibling(): return lax.ppermute(block, 'cluster', inchip)  5.03 us
    ppermute x5, waiting for transfers between devices, over_edge(): return lax.ppermute(block, 'cluster', edges)  2.35 us
  transfers between devices with their start and end apart: 8, of which 2 were waited for; matrix products, arithmetic and copies ran while one was open for 0% of the time, Pallas kernels for 45%

profile of v5, /device:TPU:20, one launch (start us, length us, event | category | flops | bytes accessed | tf_op | source)
XLA Modules:
  0.0 43.0 jit_solution(14633344290581156851)
XLA Ops:
  0.6 1.2 %shard_map.59 = bf16[256,768]{1,0:T(8,128)(2,1)S(1)} custom-call(s32[1]{0:T(128)} %bitcast.idx_ref, s32[8,128]{1,0:T(8,128)} %bitcast.4, bf16[1024,768]{1,0:T(8,128)(2,1)} %embed_ref.3), custom_call_target="tpu_custom_call" | custom-call | flops 6899999744 | bytes 1024 | tf_op jit(solution)/shard_map/pallas_call | solution.py:430
  1.8 1.9 %collective-permute-start = (bf16[256,768]{1,0:T(8,128)(2,1)S(1)}, bf16[256,768]{1,0:T(8,128)(2,1)S(1)}, u32[]{:S(2)}, u32[]{:S(2)}) collective-permute-start(bf16[256,768]{1,0:T(8,128)(2,1)S(1)} %shard_map.59), channel_id=1, source_target_pairs={{1,2},{3,4},{5,6},{7,8},{9,10},{11,12},{13,14},{2,1},{4,3},{6,5},{... | collective-permute-start | bytes 1179656 | tf_op jit(solution)/shard_map/ppermute | solution.py:460
  4.4 2.2 %shard_map.60 = (s32[8]{0:T(128)S(1)}, bf16[1040,768]{1,0:T(8,128)(2,1)S(1)}, bf16[256,768]{1,0:T(8,128)(2,1)S(1)}) custom-call(s32[1]{0:T(128)} %bitcast.idx_ref, s32[2,7]{1,0:T(2,128)} %bitcast.6, s32[1]{0:T(128)S(6)} %copy.34.count_ref, s32[8,128]{1,0:T(8,128)} %bitcast.5, bf16[1024,768]{1,0:T(8,128)(2,1)} %embed_ref.3), custom_call_target="tpu_custom_call" | custom-call | flops 16099999744 | bytes 1024 | tf_op jit(solution)/shard_map/pallas_call | solution.py:430
  6.6 1.7 %collective-permute-start.2 = (bf16[1040,768]{1,0:T(8,128)(2,1)S(1)}, bf16[1040,768]{1,0:T(8,128)(2,1)S(1)}, u32[]{:S(2)}, u32[]{:S(2)}) collective-permute-start(bf16[1040,768]{1,0:T(8,128)(2,1)S(1)} %get-tuple-element.59.x_ref), channel_id=1, source_target_pairs={{0,1},{1,0},{2,3},{3,2},{4,5},{5,4},{6,7},{7,6},{8,9},{9,8},{10,11... | collective-permute-start | bytes 4792328 | tf_op jit(solution)/shard_map/ppermute | solution.py:463
  8.3 1.7 %shard_map.61 = (f32[1024,128]{1,0:T(8,128)S(1)}, f32[1024,768]{1,0:T(8,128)S(1)}) custom-call(s32[8]{0:T(128)S(1)} %get-tuple-element.43.s, bf16[1040,768]{1,0:T(8,128)(2,1)S(1)} %get-tuple-element.59.x_ref), custom_call_target="tpu_custom_call" | custom-call | flops 34500001792 | bytes 1024 | tf_op jit(solution)/shard_map/pallas_call | solution.py:430
  10.0 2.0 %collective-permute-start.1 = (bf16[256,768]{1,0:T(8,128)(2,1)S(1)}, bf16[256,768]{1,0:T(8,128)(2,1)S(1)}, u32[]{:S(2)}, u32[]{:S(2)}) collective-permute-start(bf16[256,768]{1,0:T(8,128)(2,1)S(1)} %get-tuple-element.48), channel_id=1, source_target_pairs={{1,2},{3,4},{5,6},{7,8},{9,10},{11,12},{13,14},{2,1},{4,3},{6,5},{... | collective-permute-start | bytes 1179656 | tf_op jit(solution)/shard_map/ppermute | solution.py:460
  12.1 4.0 %shard_map.62 = (bf16[256,768]{1,0:T(8,128)(2,1)S(1)}, bf16[256,768]{1,0:T(8,128)(2,1)S(1)}, f32[1024,128]{1,0:T(8,128)S(1)}, f32[1024,768]{1,0:T(8,128)S(1)}) custom-call(s32[8]{0:T(128)S(1)} %get-tuple-element.43.s, bf16[1040,768]{1,0:T(8,128)(2,1)S(1)} %get-tuple-element.59.x_ref, ...), custom_call_target="tpu_custom_call", output_to_operand_aliasing={{2}: (2, {}), {3}: (3, {})} | custom-call | flops 14949999616 | bytes 1024 | tf_op jit(solution)/shard_map/pallas_call | solution.py:430
  16.1 0.0 collective-permute-done.q_ref.qa_ref
  16.1 1.9 %shard_map.63 = (bf16[256,768]{1,0:T(8,128)(2,1)S(1)}, f32[256,128]{1,0:T(8,128)S(1)}) custom-call(s32[8]{0:T(128)S(1)} %get-tuple-element.43.s, bf16[256,768]{1,0:T(8,128)(2,1)S(1)} %collective-permute-done.q_ref.qa_ref, bf16[1040,768]{1,0:T(8,128)(2,1)S(1)} %get-tuple-element.59.x_ref, ...), custom_call_target="tpu_custom_call", output_to_operand_aliasing={{0}: (4, {})} | custom-call | flops 11500000256 | bytes 1024 | tf_op jit(solution)/shard_map/pallas_call | solution.py:430
  18.0 1.9 %collective-permute-start.5 = (bf16[256,768]{1,0:T(8,128)(2,1)S(1)}, bf16[256,768]{1,0:T(8,128)(2,1)S(1)}, u32[]{:S(2)}, u32[]{:S(2)}) collective-permute-start(bf16[256,768]{1,0:T(8,128)(2,1)S(1)} %get-tuple-element.54), channel_id=1, source_target_pairs={{1,2},{3,4},{5,6},{7,8},{9,10},{11,12},{13,14},{2,1},{4,3},{6,5},{... | collective-permute-start | bytes 1179656 | tf_op jit(solution)/shard_map/ppermute | solution.py:460
  19.9 3.0 %shard_map.64 = (f32[1024,128]{1,0:T(8,128)S(1)}, f32[1024,768]{1,0:T(8,128)S(1)}) custom-call(s32[8]{0:T(128)S(1)} %get-tuple-element.43.s, bf16[1040,768]{1,0:T(8,128)(2,1)S(1)} %get-tuple-element.59.x_ref, bf16[1040,768]{1,0:T(8,128)(2,1)S(1)} %collective-permute-done.2.sib_ref, ...), custom_call_target="tpu_custom_call", output_to_operand_aliasing={{0}: (4, {}), {1}: (5, {})} | custom-call | flops 17250000896 | bytes 1024 | tf_op jit(solution)/shard_map/pallas_call | solution.py:430
  22.9 0.7 %collective-permute-done.1.q_ref.qb_ref = bf16[256,768]{1,0:T(8,128)(2,1)S(1)} collective-permute-done((bf16[256,768]{1,0:T(8,128)(2,1)S(1)}, bf16[256,768]{1,0:T(8,128)(2,1)S(1)}, u32[]{:S(2)}, u32[]{:S(2)}) %collective-permute-start.1) | collective-permute-done | bytes 393248 | tf_op jit(solution)/shard_map/ppermute | solution.py:460
  23.6 1.9 %shard_map.65 = (bf16[256,768]{1,0:T(8,128)(2,1)S(1)}, bf16[16,512]{1,0:T(8,128)(2,1)S(1)}) custom-call(s32[8]{0:T(128)S(1)} %get-tuple-element.43.s, bf16[256,768]{1,0:T(8,128)(2,1)S(1)} %collective-permute-done.1.q_ref.qb_ref, bf16[1040,768]{1,0:T(8,128)(2,1)S(1)} %get-tuple-element.59.x_ref, ...), custom_call_target="tpu_custom_call", output_to_operand_aliasing={{0}: (5, {})} | custom-call | flops 11500000256 | bytes 1024 | tf_op jit(solution)/shard_map/pallas_call | solution.py:430
  25.5 3.4 %collective-permute-start.3 = (bf16[256,768]{1,0:T(8,128)(2,1)S(1)}, bf16[256,768]{1,0:T(8,128)(2,1)S(1)}, u32[]{:S(2)}, u32[]{:S(2)}) collective-permute-start(bf16[256,768]{1,0:T(8,128)(2,1)S(1)} %get-tuple-element.66), channel_id=1, source_target_pairs={{1,2},{3,4},{5,6},{7,8},{9,10},{11,12},{13,14},{2,1},{4,3},{6,5},{... | collective-permute-start | bytes 1179656 | tf_op jit(solution)/shard_map/ppermute | solution.py:460
  28.9 2.1 %collective-permute-start.4 = (bf16[16,512]{1,0:T(8,128)(2,1)S(1)}, bf16[16,512]{1,0:T(8,128)(2,1)S(1)}, u32[]{:S(2)}, u32[]{:S(2)}) collective-permute-start(bf16[16,512]{1,0:T(8,128)(2,1)S(1)} %get-tuple-element.68), channel_id=1, source_target_pairs={{1,2},{3,4},{5,6},{7,8},{9,10},{11,12},{13,14},{2,1},{4,3},{6,5},{... | collective-permute-start | bytes 49160 | tf_op jit(solution)/shard_map/ppermute | solution.py:460
  31.0 3.3 %collective-permute-start.6 = (bf16[256,768]{1,0:T(8,128)(2,1)S(1)}, bf16[256,768]{1,0:T(8,128)(2,1)S(1)}, u32[]{:S(2)}, u32[]{:S(2)}) collective-permute-start(bf16[256,768]{1,0:T(8,128)(2,1)S(1)} %collective-permute-done.q_ref.qa_ref), channel_id=1, source_target_pairs={{0,1},{1,0},{2,3},{3,2},{4,5},{5,4},{6,7},{7,6},{8,9},{9,8},{10,11... | collective-permute-start | bytes 1179656 | tf_op jit(solution)/shard_map/ppermute | solution.py:463
  34.3 0.1 collective-permute-start.7
  34.4 2.6 %shard_map.66 = (s32[10]{0:T(128)S(4)}, f32[1024,128]{1,0:T(8,128)S(1)}, f32[1024,768]{1,0:T(8,128)S(1)}) custom-call(s32[8]{0:T(128)S(1)} %get-tuple-element.43.s, bf16[1040,768]{1,0:T(8,128)(2,1)S(1)} %get-tuple-element.59.x_ref, bf16[256,768]{1,0:T(8,128)(2,1)S(1)} %collective-permute-done.q_ref.qa_ref, ...), custom_call_target="tpu_custom_call", output_to_operand_aliasing={{1}: (4, {}), {2}: (5, {})} | custom-call | flops 17250000896 | bytes 1024 | tf_op jit(solution)/shard_map/pallas_call | solution.py:430
  37.0 0.0 collective-permute-done.7.fb_ref
  37.0 0.7 %shard_map.67 = (f32[1024,128]{1,0:T(8,128)S(1)}, f32[1024,768]{1,0:T(8,128)S(1)}) custom-call(s32[8]{0:T(128)S(1)} %get-tuple-element.43.s, bf16[1040,768]{1,0:T(8,128)(2,1)S(1)} %get-tuple-element.59.x_ref, bf16[1040,768]{1,0:T(8,128)(2,1)S(1)} %collective-permute-done.2.sib_ref, ...), custom_call_target="tpu_custom_call", output_to_operand_aliasing={{0}: (5, {}), {1}: (6, {})} | custom-call | flops 17250000896 | bytes 1024 | tf_op jit(solution)/shard_map/pallas_call | solution.py:430
  37.7 0.0 collective-permute-done.5.q_ref
  37.7 1.4 %shard_map.68 = (f32[8,512]{1,0:T(8,128)S(1)}, f32[8,128]{1,0:T(8,128)}, bf16[1024,768]{1,0:T(8,128)(2,1)}, f32[1024,128]{1,0:T(8,128)S(1)}, f32[1024,768]{1,0:T(8,128)S(1)}) custom-call(s32[10]{0:T(128)S(4)} %get-tuple-element.65.s, bf16[1040,768]{1,0:T(8,128)(2,1)S(1)} %get-tuple-element.59.x_ref, ...), custom_call_target="tpu_custom_call", output_to_operand_aliasing={{3}: (3, {}), {4}: (4, {})} | custom-call | flops 5750000128 | bytes 1024 | tf_op jit(solution)/shard_map/pallas_call | solution.py:430
  39.1 1.7 %collective-permute-done.4.tile_ref = bf16[16,512]{1,0:T(8,128)(2,1)S(1)} collective-permute-done((bf16[16,512]{1,0:T(8,128)(2,1)S(1)}, bf16[16,512]{1,0:T(8,128)(2,1)S(1)}, u32[]{:S(2)}, u32[]{:S(2)}) %collective-permute-start.4) | collective-permute-done | bytes 16416 | tf_op jit(solution)/shard_map/ppermute | solution.py:460
  40.8 2.0 %shard_map.69 = (f32[8,128]{1,0:T(8,128)}, bf16[1024,768]{1,0:T(8,128)(2,1)}) custom-call(s32[10]{0:T(128)S(4)} %get-tuple-element.65.s, bf16[1040,768]{1,0:T(8,128)(2,1)S(1)} %get-tuple-element.59.x_ref, bf16[256,768]{1,0:T(8,128)(2,1)S(1)} %collective-permute-done.3.q_ref, ...), custom_call_target="tpu_custom_call", output_to_operand_aliasing={{0}: (7, {}), {1}: (8, {})} | custom-call | flops 5750000128 | bytes 1024 | tf_op jit(solution)/shard_map/pallas_call | solution.py:430
  (3 shorter events, 0.0 us)
Async XLA Ops:
  1.8 14.2 %collective-permute-start = (bf16[256,768]{1,0:T(8,128)(2,1)S(1)}, bf16[256,768]{1,0:T(8,128)(2,1)S(1)}, u32[]{:S(2)}, u32[]{:S(2)}) collective-permute-start(bf16[256,768]{1,0:T(8,128)(2,1)S(1)} %shard_map.59), channel_id=1, source_target_pairs={{1,2},{3,4},{5,6},{7,8},{9,10},{11,12},{13,14},{2,1},{4,3},{6,5},{... | collective-permute-start | bytes 1179656 | tf_op jit(solution)/shard_map/ppermute | solution.py:460
  6.6 9.5 %collective-permute-start.2 = (bf16[1040,768]{1,0:T(8,128)(2,1)S(1)}, bf16[1040,768]{1,0:T(8,128)(2,1)S(1)}, u32[]{:S(2)}, u32[]{:S(2)}) collective-permute-start(bf16[1040,768]{1,0:T(8,128)(2,1)S(1)} %get-tuple-element.59.x_ref), channel_id=1, source_target_pairs={{0,1},{1,0},{2,3},{3,2},{4,5},{5,4},{6,7},{7,6},{8,9},{9,8},{10,11... | collective-permute-start | bytes 4792328 | tf_op jit(solution)/shard_map/ppermute | solution.py:463
  10.0 13.6 %collective-permute-start.1 = (bf16[256,768]{1,0:T(8,128)(2,1)S(1)}, bf16[256,768]{1,0:T(8,128)(2,1)S(1)}, u32[]{:S(2)}, u32[]{:S(2)}) collective-permute-start(bf16[256,768]{1,0:T(8,128)(2,1)S(1)} %get-tuple-element.48), channel_id=1, source_target_pairs={{1,2},{3,4},{5,6},{7,8},{9,10},{11,12},{13,14},{2,1},{4,3},{6,5},{... | collective-permute-start | bytes 1179656 | tf_op jit(solution)/shard_map/ppermute | solution.py:460
  18.0 19.7 %collective-permute-start.5 = (bf16[256,768]{1,0:T(8,128)(2,1)S(1)}, bf16[256,768]{1,0:T(8,128)(2,1)S(1)}, u32[]{:S(2)}, u32[]{:S(2)}) collective-permute-start(bf16[256,768]{1,0:T(8,128)(2,1)S(1)} %get-tuple-element.54), channel_id=1, source_target_pairs={{1,2},{3,4},{5,6},{7,8},{9,10},{11,12},{13,14},{2,1},{4,3},{6,5},{... | collective-permute-start | bytes 1179656 | tf_op jit(solution)/shard_map/ppermute | solution.py:460
  25.5 15.3 %collective-permute-start.3 = (bf16[256,768]{1,0:T(8,128)(2,1)S(1)}, bf16[256,768]{1,0:T(8,128)(2,1)S(1)}, u32[]{:S(2)}, u32[]{:S(2)}) collective-permute-start(bf16[256,768]{1,0:T(8,128)(2,1)S(1)} %get-tuple-element.66), channel_id=1, source_target_pairs={{1,2},{3,4},{5,6},{7,8},{9,10},{11,12},{13,14},{2,1},{4,3},{6,5},{... | collective-permute-start | bytes 1179656 | tf_op jit(solution)/shard_map/ppermute | solution.py:460
  28.9 11.9 %collective-permute-start.4 = (bf16[16,512]{1,0:T(8,128)(2,1)S(1)}, bf16[16,512]{1,0:T(8,128)(2,1)S(1)}, u32[]{:S(2)}, u32[]{:S(2)}) collective-permute-start(bf16[16,512]{1,0:T(8,128)(2,1)S(1)} %get-tuple-element.68), channel_id=1, source_target_pairs={{1,2},{3,4},{5,6},{7,8},{9,10},{11,12},{13,14},{2,1},{4,3},{6,5},{... | collective-permute-start | bytes 49160 | tf_op jit(solution)/shard_map/ppermute | solution.py:460
  31.0 6.0 %collective-permute-start.6 = (bf16[256,768]{1,0:T(8,128)(2,1)S(1)}, bf16[256,768]{1,0:T(8,128)(2,1)S(1)}, u32[]{:S(2)}, u32[]{:S(2)}) collective-permute-start(bf16[256,768]{1,0:T(8,128)(2,1)S(1)} %collective-permute-done.q_ref.qa_ref), channel_id=1, source_target_pairs={{0,1},{1,0},{2,3},{3,2},{4,5},{5,4},{6,7},{7,6},{8,9},{9,8},{10,11... | collective-permute-start | bytes 1179656 | tf_op jit(solution)/shard_map/ppermute | solution.py:463
  34.3 2.7 %collective-permute-start.7 = (bf16[256,768]{1,0:T(8,128)(2,1)S(1)}, bf16[256,768]{1,0:T(8,128)(2,1)S(1)}, u32[]{:S(2)}, u32[]{:S(2)}) collective-permute-start(bf16[256,768]{1,0:T(8,128)(2,1)S(1)} %collective-permute-done.1.q_ref.qb_ref), channel_id=1, source_target_pairs={{0,1},{1,0},{2,3},{3,2},{4,5},{5,4},{6,7},{7,6},{8,9},{9,8},{10,11... | collective-permute-start | bytes 1179656 | tf_op jit(solution)/shard_map/ppermute | solution.py:463
